TPU v7x, 512 devices: a whole 4x8x8 slice. The times are simulated.
512 devices in a mesh: vel: 64 (over x, y, z_lo), cell: 8 (over z_hi, core).
Axes of the slice: x: 4, y: 8, z: 8 (z_hi: 4, z_lo: 2; z = z_hi * 2 + z_lo), core: 2. Of those that a mesh axis runs over, the one named last changes fastest.
Arguments:
- state_init: float32 [13824, 16, 1024], P('vel', 'cell'), as said below
- cell_kind: int32 [16, 1024], P('cell'), may hold values from 0 to 3, as said below
- boundary_state: float32 [6], replicated, may hold values from 0.5 to 1.5
Outputs:
- state_final: float32 [13824, 16, 1024], P('vel', 'cell')
- macro: float32 [5, 16, 1024], P(None, 'cell')
Inputs may be any that keep to these rules, and one draw needn't show every extreme that they name: `state_init`: positive everywhere. `cell_kind`: the first cell plane along the nozzle axis holds only inlet and wall cells, the last plane only outlet cells.
All inputs are finite; a program needn't handle non-finite values.
Results may differ from a plain program's by a relative error of at most 0.0003.
Values sent between devices are 32-bit elements; how exact they have to be, the bound alone decides.
A program may use at most 128 MiB of HBM per device.

v0:
```python
import jax
import jax.numpy as jnp
import numpy as np
from jax import lax
from jax.sharding import PartitionSpec as P

QUAD_ABSCISSAE = 24
NZ = 32
STEPS = 2


MOMENTUM_RATIO = 2.0 / 3.0
SHEAR_EXPONENT = 0.81
SHEAR_REFERENCE = 0.05
TIME_INCREMENT = 0.03125


def extended(cells, sides, width):
    for axis, dim in sides:
        count = lax.axis_size(axis)
        ends = count - 1
        head = lax.slice_in_dim(cells, 0, width, axis=dim)
        tail = lax.slice_in_dim(cells, cells.shape[dim] - width, cells.shape[dim], axis=dim)
        cells = jnp.concatenate(
            [
                lax.ppermute(tail, axis, [(i, (i + 1) % count) for i in range(ends)]),
                cells,
                lax.ppermute(head, axis, [((i + 1) % count, i) for i in range(ends)]),
            ],
            axis=dim,
        )
    return cells


def hermite_rule(points):
    start_value = np.pi ** (-0.25)
    node_list = np.zeros(points)
    weight_list = np.zeros(points)
    guess_root = 0.0
    slope_value = 1.0
    for index in range((points + 1) // 2):
        if index == 0:
            guess_root = np.sqrt(2.0 * points + 1.0) - 1.85575 * (2.0 * points + 1.0) ** (-0.16667)
        elif index == 1:
            guess_root = guess_root - 1.14 * points**0.426 / guess_root
        elif index == 2:
            guess_root = 1.86 * guess_root - 0.86 * node_list[0]
        elif index == 3:
            guess_root = 1.91 * guess_root - 0.91 * node_list[1]
        else:
            guess_root = 2.0 * guess_root - node_list[index - 2]
        for sweep in range(60):
            poly_now = start_value
            poly_prev = 0.0
            for degree in range(points):
                poly_old = poly_prev
                poly_prev = poly_now
                poly_now = (
                    guess_root * np.sqrt(2.0 / (degree + 1)) * poly_prev
                    - np.sqrt(degree / (degree + 1.0)) * poly_old
                )
            slope_value = np.sqrt(2.0 * points) * poly_prev
            guess_root = guess_root - poly_now / slope_value
        node_list[index] = guess_root
        node_list[points - 1 - index] = -guess_root
        weight_list[index] = 2.0 / (slope_value * slope_value)
        weight_list[points - 1 - index] = weight_list[index]
    return (node_list[::-1].copy(), weight_list[::-1].copy())


def node_order(points):
    stride = points // 4
    pieces = np.meshgrid(
        np.arange(4),
        np.arange(4),
        np.arange(4),
        np.arange(stride),
        np.arange(stride),
        np.arange(stride),
        indexing="ij",
    )
    return [
        (4 * pieces[3 + axis_number] + pieces[axis_number]).reshape(-1) for axis_number in range(3)
    ]


def node_table(points):
    abscissa, weights = hermite_rule(points)
    one_dimensional_abscissae = np.sqrt(2.0) * abscissa
    weights_one = weights * np.exp(abscissa * abscissa) / np.sqrt(np.pi)
    order_a, order_b, order_c = node_order(points)
    speeds = np.stack(
        [
            one_dimensional_abscissae[order_a],
            one_dimensional_abscissae[order_b],
            one_dimensional_abscissae[order_c],
        ]
    )
    quadrature = weights_one[order_a] * weights_one[order_b] * weights_one[order_c]
    return (speeds, quadrature)


def moment_rows(speeds, quadrature):
    speed_x, speed_y, speed_z = (speeds[0], speeds[1], speeds[2])
    square = speed_x * speed_x + speed_y * speed_y + speed_z * speed_z
    return np.stack(
        [
            quadrature,
            quadrature * speed_x,
            quadrature * speed_y,
            quadrature * speed_z,
            quadrature * speed_x * speed_x,
            quadrature * speed_y * speed_y,
            quadrature * speed_z * speed_z,
            quadrature * speed_x * speed_y,
            quadrature * speed_x * speed_z,
            quadrature * speed_y * speed_z,
            quadrature * speed_x * square,
            quadrature * speed_y * square,
            quadrature * speed_z * square,
        ]
    )


def equilibrium_fields(moments):
    particle_concentration = moments[0]
    first = (moments[1], moments[2], moments[3])
    mean_flow_vector = (
        first[0] / particle_concentration,
        first[1] / particle_concentration,
        first[2] / particle_concentration,
    )
    diagonal_tensor_total = moments[4] + moments[5] + moments[6]
    lattice_magnitude_squared = (
        mean_flow_vector[0] * mean_flow_vector[0]
        + mean_flow_vector[1] * mean_flow_vector[1]
        + mean_flow_vector[2] * mean_flow_vector[2]
    )
    thermal_level = (
        diagonal_tensor_total / particle_concentration - lattice_magnitude_squared
    ) / 3.0
    pairs = ((4, 7, 8), (7, 5, 9), (8, 9, 6))
    along = (
        mean_flow_vector[0] * first[0]
        + mean_flow_vector[1] * first[1]
        + mean_flow_vector[2] * first[2]
    )
    energy_current_vectors = []
    for coordinate_choice in range(3):
        tensor_part = (
            moments[pairs[coordinate_choice][0]] * mean_flow_vector[0]
            + moments[pairs[coordinate_choice][1]] * mean_flow_vector[1]
            + moments[pairs[coordinate_choice][2]] * mean_flow_vector[2]
        )
        energy_current_vectors.append(
            0.5
            * (
                moments[10 + coordinate_choice]
                - 2.0 * tensor_part
                + lattice_magnitude_squared * first[coordinate_choice]
                - mean_flow_vector[coordinate_choice] * diagonal_tensor_total
                + 2.0 * mean_flow_vector[coordinate_choice] * along
                - mean_flow_vector[coordinate_choice]
                * lattice_magnitude_squared
                * particle_concentration
            )
        )
    return jnp.stack(
        [
            particle_concentration,
            mean_flow_vector[0],
            mean_flow_vector[1],
            mean_flow_vector[2],
            thermal_level,
            energy_current_vectors[0],
            energy_current_vectors[1],
            energy_current_vectors[2],
        ]
    )


def transport(padded, speeds, depth_z):
    center = padded[:, 1:-1]
    speed_x = speeds[0][:, None, None]
    speed_y = speeds[1][:, None, None]
    speed_z = speeds[2][:, None, None]
    grad_x = jnp.where(speed_x > 0, center - padded[:, :-2], padded[:, 2:] - center)
    mixed_products = center.shape[2]
    zeros_one = jnp.zeros(center.shape[:2] + (1,), center.dtype)
    zeros_row = jnp.zeros(center.shape[:2] + (depth_z,), center.dtype)
    z_index = lax.broadcasted_iota(jnp.int32, (1, 1, mixed_products), 2) % depth_z
    below_z = jnp.where(z_index == 0, 0.0, jnp.concatenate([zeros_one, center[..., :-1]], 2))
    above_z = jnp.where(
        z_index == depth_z - 1, 0.0, jnp.concatenate([center[..., 1:], zeros_one], 2)
    )
    below_y = jnp.concatenate([zeros_row, center[..., :-depth_z]], 2)
    above_y = jnp.concatenate([center[..., depth_z:], zeros_row], 2)
    grad_y = jnp.where(speed_y > 0, center - below_y, above_y - center)
    grad_z = jnp.where(speed_z > 0, center - below_z, above_z - center)
    return center - TIME_INCREMENT * (speed_x * grad_x + speed_y * grad_y + speed_z * grad_z)


def relax(moved, moment_quantities, kinds, speeds, boundary):
    particle_concentration, thermal_level = (moment_quantities[0], moment_quantities[4])
    mean_flow_vector = (moment_quantities[1], moment_quantities[2], moment_quantities[3])
    heat = (moment_quantities[5], moment_quantities[6], moment_quantities[7])
    comps = [
        speeds[coordinate_choice][:, None, None] - mean_flow_vector[coordinate_choice]
        for coordinate_choice in range(3)
    ]
    relative_magnitude_squared = comps[0] * comps[0] + comps[1] * comps[1] + comps[2] * comps[2]
    isotropic_load = particle_concentration * thermal_level
    equilibrium_profile = (
        particle_concentration
        * thermal_level ** (-1.5)
        * jnp.exp(-relative_magnitude_squared / (2.0 * thermal_level))
    )
    energy_current_projection = comps[0] * heat[0] + comps[1] * heat[1] + comps[2] * heat[2]
    corrected_equilibrium = equilibrium_profile * (
        1.0
        + (1.0 - MOMENTUM_RATIO)
        * energy_current_projection
        * (relative_magnitude_squared / thermal_level - 5.0)
        / (5.0 * isotropic_load * thermal_level)
    )
    relaxation_frequency = (
        TIME_INCREMENT * isotropic_load / (SHEAR_REFERENCE * thermal_level**SHEAR_EXPONENT)
    )
    relaxed = (moved + relaxation_frequency * corrected_equilibrium) / (1.0 + relaxation_frequency)
    node_sq = (speeds[0] * speeds[0] + speeds[1] * speeds[1] + speeds[2] * speeds[2])[:, None, None]
    wall_temp = boundary[5]
    wall = particle_concentration * wall_temp ** (-1.5) * jnp.exp(-node_sq / (2.0 * wall_temp))
    inlet_sq = (
        (speeds[0] - boundary[1]) ** 2
        + (speeds[1] - boundary[2]) ** 2
        + (speeds[2] - boundary[3]) ** 2
    )[:, None, None]
    inlet = boundary[0] * boundary[4] ** (-1.5) * jnp.exp(-inlet_sq / (2.0 * boundary[4]))
    return jnp.where(
        kinds == 0, relaxed, jnp.where(kinds == 1, wall, jnp.where(kinds == 2, inlet, moved))
    )


def shards(state_init, cell_kind, boundary_state):
    count = state_init.shape[0]
    mixed_products = state_init.shape[2]
    speeds_np, quadrature = node_table(QUAD_ABSCISSAE)
    first_node = lax.axis_index("vel") * count
    speeds = lax.dynamic_slice_in_dim(jnp.asarray(speeds_np, jnp.float32), first_node, count, 1)
    weights = lax.dynamic_slice_in_dim(
        jnp.asarray(moment_rows(speeds_np, quadrature), jnp.float32), first_node, count, 1
    )

    def cell_fields(moved):
        depth = moved.shape[1]
        moments = jnp.dot(
            weights, moved.reshape(count, depth * mixed_products), precision=lax.Precision.HIGHEST
        )
        moment_quantities = equilibrium_fields(lax.psum(moments, "vel"))
        return moment_quantities.reshape(8, depth, mixed_products)

    particle_population = state_init
    for section in range(STEPS):
        padded = extended(particle_population, (("cell", 1),), 1)
        moved = transport(padded, speeds, NZ)
        moment_quantities = cell_fields(moved)
        particle_population = relax(moved, moment_quantities, cell_kind, speeds, boundary_state)
    final = cell_fields(particle_population)
    return (particle_population, final[:5])


def solution(mesh):
    in_specs = (P("vel", "cell", None), P("cell", None), P())
    out_specs = (P("vel", "cell", None), P(None, "cell", None))
    return jax.shard_map(shards, mesh=mesh, in_specs=in_specs, out_specs=out_specs, check_vma=False)
```

profile of v0, /device:TPU:1, one launch (start us, length us, event | category | flops | bytes accessed | tf_op | source)
XLA Modules:
  0.0 1683.8 jit_solution(2789155993239934769)
XLA Ops:
  7.2 2.0 copy.37
  10.6 7.2 collective-permute-start
  17.8 2.9 collective-permute-start.1
  22.4 1.6 fusion.89
  28.1 14.6 collective-permute-done.1
  43.7 3.7 fusion.52
  47.5 2.4 fusion.58
  50.0 1.9 divide_exponential_fusion
  52.6 507.0 %all-reduce.12.cloned.1.call-done = f32[13,2048]{1,0:T(8,128)} async-done(((f32[13,2048]{1,0:T(8,128)}), f32[13,2048]{1,0:T(8,128)}) %all-reduce.12.cloned.1.call-update) | async-done | bytes 106512 | tf_op jit(solution)/shard_map/psum | solution.py:259
  561.5 2.0 fusion.82
  565.0 3.1 fusion.18
  568.3 35.3 %collective-permute-start.2 = (f32[216,1,1024]{2,0,1:T(8,128)S(1)}, f32[216,1,1024]{2,0,1:T(8,128)S(1)}, u32[]{:S(2)}, u32[]{:S(2)}) collective-permute-start(f32[216,1,1024]{2,0,1:T(8,128)S(1)} %get-tuple-element.52), channel_id=1, source_target_pairs={{0,1},{1,2},{2,3},{3,4},{4,5},{5,6},{6,7},{8,9},{9,10},{10,11},{11... | collective-permute-start | bytes 2654216 | tf_op jit(solution)/shard_map/ppermute | solution.py:26
  603.6 2.1 collective-permute-start.3
  607.1 6.5 collective-permute-done.2
  613.6 14.7 collective-permute-done.3
  628.4 2.5 fusion.44
  631.0 2.4 fusion.56
  633.4 499.0 %all-reduce.14.cloned.1.call-done = f32[13,2048]{1,0:T(8,128)} async-done(((f32[13,2048]{1,0:T(8,128)}), f32[13,2048]{1,0:T(8,128)}) %all-reduce.14.cloned.1.call-update) | async-done | bytes 106512 | tf_op jit(solution)/shard_map/psum | solution.py:259
  1135.2 2.0 fusion.81
  1137.4 3.0 fusion.93
  1140.6 2.4 fusion.54
  1143.0 2.9 fusion.37
  1145.9 2.6 copy.41
  1148.5 526.9 %all-reduce.16.cloned.1.call-done = f32[13,2048]{1,0:T(8,128)} async-done(((f32[13,2048]{1,0:T(8,128)}), f32[13,2048]{1,0:T(8,128)}) %all-reduce.16.cloned.1.call-update) | async-done | bytes 106512 | tf_op jit(solution)/shard_map/psum | solution.py:259
  (87 shorter events, 15.7 us)
Async XLA Ops:
  7.2 552.4 %all-reduce.12.cloned.1.call-start = ((), (), s32[]{:S(2)}) async-start(), calls=%async_computation | async-start | bytes 262144 | tf_op jit(solution)/shard_map/psum | solution.py:259
  10.6 17.5 %collective-permute-start = (f32[216,1,1024]{2,0,1:T(8,128)}, f32[216,1,1024]{2,0,1:T(8,128)S(1)}, u32[]{:S(2)}, u32[]{:S(2)}) collective-permute-start(f32[216,1,1024]{2,0,1:T(8,128)} %get-tuple-element.58), channel_id=1, source_target_pairs={{0,1},{1,2},{2,3},{3,4},{4,5},{5,6},{6,7},{8,9},{9,10},{10,11},{11... | collective-permute-start | bytes 2654216 | tf_op jit(solution)/shard_map/ppermute | solution.py:26
  17.8 25.0 %collective-permute-start.1 = (f32[216,1,1024]{2,0,1:T(8,128)}, f32[216,1,1024]{2,0,1:T(8,128)S(1)}, u32[]{:S(2)}, u32[]{:S(2)}) collective-permute-start(f32[216,1,1024]{2,0,1:T(8,128)} %get-tuple-element.59), channel_id=1, source_target_pairs={{1,0},{2,1},{3,2},{4,3},{5,4},{6,5},{7,6},{9,8},{10,9},{11,10},{12... | collective-permute-start | bytes 2654216 | tf_op jit(solution)/shard_map/ppermute | solution.py:28
  21.6 22.0 %copy-start.2 = (f32[1,216]{1,0:T(1,128)}, f32[1,216]{1,0:T(1,128)S(1)}, u32[]{:S(2)}) copy-start(f32[1,216]{1,0:T(1,128)S(1)} %get-tuple-element.62) | copy-start | bytes 2596
  21.6 22.0 %copy-start.4 = (f32[1,216]{1,0:T(1,128)}, f32[1,216]{1,0:T(1,128)S(1)}, u32[]{:S(2)}) copy-start(f32[1,216]{1,0:T(1,128)S(1)} %get-tuple-element.60) | copy-start | bytes 2596
  21.6 22.0 %copy-start.14 = (pred[216]{0:T(512)(128)(4,1)}, pred[216]{0:T(512)(128)(4,1)S(1)}, u32[]{:S(2)}) copy-start(pred[216]{0:T(512)(128)(4,1)S(1)} %broadcast_compare_fusion.5) | copy-start | bytes 652
  22.4 21.3 %copy-start.10 = (pred[216]{0:T(512)(128)(4,1)}, pred[216]{0:T(512)(128)(4,1)S(1)}, u32[]{:S(2)}) copy-start(pred[216]{0:T(512)(128)(4,1)S(1)} %get-tuple-element.85) | copy-start | bytes 652
  22.4 21.3 %copy-start.12 = (pred[216]{0:T(512)(128)(4,1)}, pred[216]{0:T(512)(128)(4,1)S(1)}, u32[]{:S(2)}) copy-start(pred[216]{0:T(512)(128)(4,1)S(1)} %get-tuple-element.86) | copy-start | bytes 652
  26.7 17.0 %copy-start.6 = (pred[1024]{0:T(1024)(128)(4,1)}, pred[1024]{0:T(1024)(128)(4,1)S(1)}, u32[]{:S(2)}) copy-start(pred[1024]{0:T(1024)(128)(4,1)S(1)} %get-tuple-element.83) | copy-start | bytes 3076
  26.7 17.0 %copy-start.8 = (pred[1024]{0:T(1024)(128)(4,1)}, pred[1024]{0:T(1024)(128)(4,1)S(1)}, u32[]{:S(2)}) copy-start(pred[1024]{0:T(1024)(128)(4,1)S(1)} %get-tuple-element.84) | copy-start | bytes 3076
  28.1 14.6 copy-start
  42.7 0.9 copy-start.1
  47.5 2.5 copy-start.3
  47.5 2.5 copy-start.5
  49.9 1082.5 %all-reduce.14.cloned.1.call-start = ((), (), s32[]{:S(2)}) async-start(), calls=%async_computation.1 | async-start | bytes 262144 | tf_op jit(solution)/shard_map/psum | solution.py:259
  568.3 45.3 %collective-permute-start.2 = (f32[216,1,1024]{2,0,1:T(8,128)S(1)}, f32[216,1,1024]{2,0,1:T(8,128)S(1)}, u32[]{:S(2)}, u32[]{:S(2)}) collective-permute-start(f32[216,1,1024]{2,0,1:T(8,128)S(1)} %get-tuple-element.52), channel_id=1, source_target_pairs={{0,1},{1,2},{2,3},{3,4},{4,5},{5,6},{6,7},{8,9},{9,10},{10,11},{11... | collective-permute-start | bytes 2654216 | tf_op jit(solution)/shard_map/ppermute | solution.py:26
  603.6 24.7 %collective-permute-start.3 = (f32[216,1,1024]{2,0,1:T(8,128)S(1)}, f32[216,1,1024]{2,0,1:T(8,128)S(1)}, u32[]{:S(2)}, u32[]{:S(2)}) collective-permute-start(f32[216,1,1024]{2,0,1:T(8,128)S(1)} %get-tuple-element.53), channel_id=1, source_target_pairs={{1,0},{2,1},{3,2},{4,3},{5,4},{6,5},{7,6},{9,8},{10,9},{11,10},{12... | collective-permute-start | bytes 2654216 | tf_op jit(solution)/shard_map/ppermute | solution.py:28
  606.4 21.9 %copy-start.7 = (pred[1024]{0:T(1024)(128)(4,1)S(1)}, pred[1024]{0:T(1024)(128)(4,1)}, u32[]{:S(2)}) copy-start(pred[1024]{0:T(1024)(128)(4,1)} %copy-done.6) | copy-start | bytes 3076
  606.4 21.9 %copy-start.9 = (pred[1024]{0:T(1024)(128)(4,1)S(1)}, pred[1024]{0:T(1024)(128)(4,1)}, u32[]{:S(2)}) copy-start(pred[1024]{0:T(1024)(128)(4,1)} %copy-done.8) | copy-start | bytes 3076
  606.4 21.9 %copy-start.11 = (pred[216]{0:T(512)(128)(4,1)S(1)}, pred[216]{0:T(512)(128)(4,1)}, u32[]{:S(2)}) copy-start(pred[216]{0:T(512)(128)(4,1)} %copy-done.10) | copy-start | bytes 652
  606.4 21.9 %copy-start.13 = (pred[216]{0:T(512)(128)(4,1)S(1)}, pred[216]{0:T(512)(128)(4,1)}, u32[]{:S(2)}) copy-start(pred[216]{0:T(512)(128)(4,1)} %copy-done.12) | copy-start | bytes 652
  606.4 21.9 %copy-start.15 = (pred[216]{0:T(512)(128)(4,1)S(1)}, pred[216]{0:T(512)(128)(4,1)}, u32[]{:S(2)}) copy-start(pred[216]{0:T(512)(128)(4,1)} %copy-done.14) | copy-start | bytes 652
  633.4 1042.0 %all-reduce.16.cloned.1.call-start = ((), (), s32[]{:S(2)}) async-start(), calls=%async_computation.2 | async-start | bytes 262144 | tf_op jit(solution)/shard_map/psum | solution.py:259
Sparse Core Ops, SparseCore 0:
  50.1 509.4 all-reduce.11
  633.5 498.9 all-reduce.13
  1143.1 532.2 all-reduce.15
where the time goes:
time: 1710 us; the launch traced here: 1680 us
  waiting for transfers between devices  1570 us (92%)
  starting transfers between devices  47.6 us (3%)
  other arithmetic  28.5 us (2%)
  between operations  17.7 us (1%)
    psum x3, waiting for transfers between devices, cell_fields(): moment_quantities = equilibrium_fields(lax.psum(moments, 'vel'))  1530 us
    ppermute x2, starting transfers between devices, extended(): lax.ppermute(tail, axis, [(i, (i + 1) % count) for i in range(ends)])  42.5 us
  transfers between devices with their start and end apart: 7, of which 6 were waited for; matrix products, arithmetic and copies ran while one was open for 1% of the time, Pallas kernels for 0%

commit v1 on v0

--- a/solution.py
+++ b/solution.py
@@ -2,6 +2,8 @@
 import jax.numpy as jnp
 import numpy as np
 from jax import lax
+from jax.experimental import pallas as pl
+from jax.experimental.pallas import tpu as pltpu
 from jax.sharding import PartitionSpec as P
 
 QUAD_ABSCISSAE = 24
@@ -241,6 +243,88 @@
     )
 
 
+MESH = pl.DeviceIdType.MESH
+
+
+def sum_kernel(part_ref, out_ref, got_a, mine, got_b, send_sem, recv_sem):
+    vel = lax.axis_index("vel")
+    cell = lax.axis_index("cell")
+    lo = lax.rem(vel, 2)
+    row = lax.rem(vel // 2, 8)
+    col = vel // 16
+    here = col * 2 + lo
+
+    def peer_a(other):
+        return ((other // 2) * 16 + row * 2 + lax.rem(other, 2), cell)
+
+    def peer_b(other):
+        return (col * 16 + other * 2 + lo, cell)
+
+    barrier = pltpu.get_barrier_semaphore()
+    for k in range(1, 8):
+        pl.semaphore_signal(barrier, inc=1, device_id=peer_a(lax.rem(here + k, 8)), device_id_type=MESH)
+        pl.semaphore_signal(barrier, inc=1, device_id=peer_b(lax.rem(row + k, 8)), device_id_type=MESH)
+    pl.semaphore_wait(barrier, 14)
+
+    def exchange(phase, source, target, index, peer):
+        copies = []
+        for k in range(1, 8):
+            other = lax.rem(index + k, 8)
+            copy = pltpu.make_async_remote_copy(
+                src_ref=source(other),
+                dst_ref=target,
+                send_sem=send_sem.at[phase, k - 1],
+                recv_sem=recv_sem.at[phase, k - 1],
+                device_id=peer(other),
+                device_id_type=MESH,
+            )
+            copy.start()
+            copies.append(copy)
+        return copies
+
+    copies = exchange(0, lambda other: part_ref.at[other], got_a.at[here], here, peer_a)
+    got_a[here] = part_ref[here]
+    for copy in copies:
+        copy.wait()
+    total = got_a[0]
+    for k in range(1, 8):
+        total = total + got_a[k]
+    mine[...] = total
+    copies = exchange(1, lambda other: mine, got_b.at[row], row, peer_b)
+    got_b[row] = total
+    for copy in copies:
+        copy.wait()
+    total = got_b[0]
+    for k in range(1, 8):
+        total = total + got_b[k]
+    out_ref[here] = total
+    copies = exchange(2, lambda other: out_ref.at[here], out_ref.at[here], here, peer_a)
+    for copy in copies:
+        copy.wait()
+
+
+def summed(moments):
+    rows, cells = moments.shape
+    parts = jnp.pad(moments, ((0, 16 - rows), (0, 0))).reshape(16, 2, 8, 128)
+    parts = parts.transpose(2, 0, 1, 3).reshape(8, 32, 128)
+    total = pl.pallas_call(
+        sum_kernel,
+        out_shape=jax.ShapeDtypeStruct((8, 32, 128), jnp.float32),
+        in_specs=[pl.BlockSpec(memory_space=pltpu.VMEM)],
+        out_specs=pl.BlockSpec(memory_space=pltpu.VMEM),
+        scratch_shapes=[
+            pltpu.VMEM((8, 32, 128), jnp.float32),
+            pltpu.VMEM((32, 128), jnp.float32),
+            pltpu.VMEM((8, 32, 128), jnp.float32),
+            pltpu.SemaphoreType.DMA((3, 7)),
+            pltpu.SemaphoreType.DMA((3, 7)),
+        ],
+        compiler_params=pltpu.CompilerParams(collective_id=0, has_side_effects=True),
+    )(parts)
+    total = total.reshape(8, 16, 2, 128).transpose(1, 2, 0, 3)
+    return total.reshape(16, cells)[:rows]
+
+
 def shards(state_init, cell_kind, boundary_state):
     count = state_init.shape[0]
     mixed_products = state_init.shape[2]
@@ -256,7 +340,7 @@
         moments = jnp.dot(
             weights, moved.reshape(count, depth * mixed_products), precision=lax.Precision.HIGHEST
         )
-        moment_quantities = equilibrium_fields(lax.psum(moments, "vel"))
+        moment_quantities = equilibrium_fields(summed(moments))
         return moment_quantities.reshape(8, depth, mixed_products)
 
     particle_population = state_init

time: 1710 us -> 164 us (0.10)
  the two profiles are of different devices: /device:TPU:1 before, /device:TPU:256 now
where the time goes in v1:
time: 164 us; the launch traced here: 162 us
  Pallas kernels  63.8 us (39%)
  waiting for transfers between devices  29.6 us (18%)
  other arithmetic  28.5 us (17%)
  local copies, waits for them, and re-layouts  15.5 us (9%)
  starting transfers between devices  15.3 us (9%)
  matrix products  5.15 us (3%)
  between operations  4.4 us (3%)
    pallas_call x3, Pallas kernels, summed(): pl.pallas_call(sum_kernel, out_shape=jax.ShapeDtypeStruct((8, 32, 128), j...  63.8 us
    ppermute x2, waiting for transfers between devices, extended(): lax.ppermute(tail, axis, [(i, (i + 1) % count) for i in range(ends)])  26 us
    ppermute x2, starting transfers between devices, extended(): lax.ppermute(head, axis, [((i + 1) % count, i) for i in range(ends)])  11.5 us
    unnamed x57, local copies, waits for them, and re-layouts  7.06 us
    sub x2, other arithmetic, transport(): center - TIME_INCREMENT * (speed_x * grad_x + speed_y * grad_y + speed_z...  6.42 us
    select_n x2, other arithmetic, relax(): jnp.where(kinds == 0, relaxed, jnp.where(kinds == 1, wall, jnp.where(kind...  5.97 us
    unnamed x4, other arithmetic  5.25 us
    dot_general x3, matrix products, cell_fields(): jnp.dot(weights, moved.reshape(count, depth * mixed_products), precision=...  5.15 us
  transfers between devices with their start and end apart: 4, of which 4 were waited for; matrix products, arithmetic and copies ran while one was open for 5% of the time, Pallas kernels for 0%

profile of v1, /device:TPU:256, one launch (start us, length us, event | category | flops | bytes accessed | tf_op | source)
XLA Modules:
  0.0 162.2 jit_solution(12765525868658285159)
XLA Ops:
  0.6 2.0 %copy.53 = f32[216,2,1024]{2,0,1:T(8,128)S(1)} copy(f32[216,2,1024]{2,1,0:T(2,128)} %param.5) | data formatting | bytes 3538944 | tf_op args[0]
  2.7 1.4 fusion.130
  4.1 1.9 %collective-permute-start = (f32[216,1,1024]{2,0,1:T(8,128)}, f32[216,1,1024]{2,0,1:T(8,128)S(1)}, u32[]{:S(2)}, u32[]{:S(2)}) collective-permute-start(f32[216,1,1024]{2,0,1:T(8,128)} %get-tuple-element.32), channel_id=1, source_target_pairs={{0,1},{1,2},{2,3},{3,4},{4,5},{5,6},{6,7},{8,9},{9,10},{10,11},{11... | collective-permute-start | bytes 2654216 | tf_op jit(solution)/shard_map/ppermute | solution.py:28
  6.0 5.8 %collective-permute-start.1 = (f32[216,1,1024]{2,0,1:T(8,128)}, f32[216,1,1024]{2,0,1:T(8,128)S(1)}, u32[]{:S(2)}, u32[]{:S(2)}) collective-permute-start(f32[216,1,1024]{2,0,1:T(8,128)} %get-tuple-element.33), channel_id=1, source_target_pairs={{1,0},{2,1},{3,2},{4,3},{5,4},{6,5},{7,6},{9,8},{10,9},{11,10},{12... | collective-permute-start | bytes 2654216 | tf_op jit(solution)/shard_map/ppermute | solution.py:30
  16.7 2.4 %divide_exponential_fusion = (f32[216]{0:T(256)}, f32[216]{0:T(256)}) fusion(f32[216]{0:T(256)S(1)} %bitcast.446, f32[216]{0:T(256)S(1)} %bitcast.439, f32[216]{0:T(256)S(1)} %bitcast.452, f32[]{:T(128)} %bitcast.22, f32[]{:T(128)} %bitcast.27, f32[]{:T(128)} %bitcast.26, f32[]{:T(128)} %bitcast.25, f32[]{:T(128)} %bitcast.24, f32[]{:T(128)} %bitcast.23), kind=kLoop, calls=%fused_computation.196 | loop fusion | flops 3888 | bytes 4344 | tf_op jit(solution)/shard_map/exp | solution.py:234
  21.1 9.2 %collective-permute-done = f32[216,1,1024]{2,0,1:T(8,128)S(1)} collective-permute-done((f32[216,1,1024]{2,0,1:T(8,128)}, f32[216,1,1024]{2,0,1:T(8,128)S(1)}, u32[]{:S(2)}, u32[]{:S(2)}) %collective-permute-start) | collective-permute-done | bytes 884768 | tf_op jit(solution)/shard_map/ppermute | solution.py:28
  30.3 1.8 %collective-permute-done.1 = f32[216,1,1024]{2,0,1:T(8,128)S(1)} collective-permute-done((f32[216,1,1024]{2,0,1:T(8,128)}, f32[216,1,1024]{2,0,1:T(8,128)S(1)}, u32[]{:S(2)}, u32[]{:S(2)}) %collective-permute-start.1) | collective-permute-done | bytes 884768 | tf_op jit(solution)/shard_map/ppermute | solution.py:30
  32.1 0.9 copy-done.1
  33.1 3.8 %fusion.52 = f32[216,2,1024]{2,0,1:T(8,128)S(1)} fusion(f32[216,2,1024]{2,0,1:T(8,128)S(1)} %copy.53, f32[216,1,1024]{2,0,1:T(8,128)} %copy-done.1, f32[216,1,1024]{2,0,1:T(8,128)} %copy-done, f32[216,2,1023]{2,0,1:T(8,128)S(1)} %get-tuple-element.31, f32[216,2,1023]{2,0,1:T(8,128)S(1)} %get-tuple-element.30, f32[216,2,992]{2,0,1:T(8,128)S(1)} %get-tuple-element.29, ...), kind=kLoop, calls=%fused_computation.67 | loop fusion | flops 8847360 | bytes 12277544 | tf_op jit(solution)/shard_map/sub | solution.py:202
  37.1 1.7 %fusion.58 = f32[13,2048]{1,0:T(8,128)S(1)} fusion(f32[216,2048]{1,0:T(8,128)S(1)} %bitcast.417, f32[13,13824]{1,0:T(8,128)} %constant.88.clone, s32[]{:T(128)S(6)} %select_n.79), kind=kOutput, calls=%fused_computation.77 | convolution fusion | flops 69009408 | bytes 1892356 | tf_op jit(solution)/shard_map/dot_general | solution.py:340
  39.6 24.2 %shard_map.68 = f32[8,32,128]{2,1,0:T(8,128)} custom-call(f32[8,32,128]{2,1,0:T(8,128)} %bitcast.428), custom_call_target="tpu_custom_call" | custom-call | tf_op jit(solution)/shard_map/pallas_call | solution.py:310
  67.3 3.0 %fusion.18 = f32[216,2,1024]{2,0,1:T(8,128)S(1)} fusion(f32[216,2,1024]{2,0,1:T(8,128)S(1)} %fusion.52, f32[216]{0:T(256)S(1)} %copy-done.11, f32[216]{0:T(256)S(1)} %copy-done.9, f32[2,1024]{1,0:T(2,128)S(1)} %get-tuple-element.44, f32[2,1024]{1,0:T(2,128)S(1)} %get-tuple-element.20, f32[2,1024]{1,0:T(2,128)S(1)} %get-tuple-element.38, ...), kind=kLoop, calls=%fused_computation.30 | loop fusion | flops 13271040 | bytes 3655904 | tf_op jit(solution)/shard_map/jit(_where)/select_n | solution.py:241
  70.5 1.9 %collective-permute-start.2 = (f32[216,1,1024]{2,0,1:T(8,128)S(1)}, f32[216,1,1024]{2,0,1:T(8,128)S(1)}, u32[]{:S(2)}, u32[]{:S(2)}) collective-permute-start(f32[216,1,1024]{2,0,1:T(8,128)S(1)} %get-tuple-element.26), channel_id=1, source_target_pairs={{0,1},{1,2},{2,3},{3,4},{4,5},{5,6},{6,7},{8,9},{9,10},{10,11},{11... | collective-permute-start | bytes 2654216 | tf_op jit(solution)/shard_map/ppermute | solution.py:28
  72.4 5.8 %collective-permute-start.3 = (f32[216,1,1024]{2,0,1:T(8,128)S(1)}, f32[216,1,1024]{2,0,1:T(8,128)S(1)}, u32[]{:S(2)}, u32[]{:S(2)}) collective-permute-start(f32[216,1,1024]{2,0,1:T(8,128)S(1)} %get-tuple-element.27), channel_id=1, source_target_pairs={{1,0},{2,1},{3,2},{4,3},{5,4},{6,5},{7,6},{9,8},{10,9},{11,10},{12... | collective-permute-start | bytes 2654216 | tf_op jit(solution)/shard_map/ppermute | solution.py:30
  79.7 16.8 %collective-permute-done.2 = f32[216,1,1024]{2,0,1:T(8,128)S(1)} collective-permute-done((f32[216,1,1024]{2,0,1:T(8,128)S(1)}, f32[216,1,1024]{2,0,1:T(8,128)S(1)}, u32[]{:S(2)}, u32[]{:S(2)}) %collective-permute-start.2) | collective-permute-done | bytes 884768 | tf_op jit(solution)/shard_map/ppermute | solution.py:28
  96.4 1.8 %collective-permute-done.3 = f32[216,1,1024]{2,0,1:T(8,128)S(1)} collective-permute-done((f32[216,1,1024]{2,0,1:T(8,128)S(1)}, f32[216,1,1024]{2,0,1:T(8,128)S(1)}, u32[]{:S(2)}, u32[]{:S(2)}) %collective-permute-start.3) | collective-permute-done | bytes 884768 | tf_op jit(solution)/shard_map/ppermute | solution.py:30
  98.3 2.7 %fusion.44 = f32[216,2,1024]{2,0,1:T(8,128)S(1)} fusion(f32[216,2,1024]{2,0,1:T(8,128)S(1)} %fusion.18, f32[216,1,1024]{2,0,1:T(8,128)S(1)} %collective-permute-done.3, f32[216,1,1024]{2,0,1:T(8,128)S(1)} %collective-permute-done.2, f32[216,2,1023]{2,0,1:T(8,128)S(1)} %get-tuple-element.25, f32[216,2,1023]{2,0,1:T(8,128)S(1)} %get-tuple-element.24, ...), kind=kLoop, calls=%fused_computation.57 | loop fusion | flops 8847360 | bytes 12277544 | tf_op jit(solution)/shard_map/sub | solution.py:202
  101.1 1.7 %fusion.56 = f32[13,2048]{1,0:T(8,128)S(1)} fusion(f32[216,2048]{1,0:T(8,128)S(1)} %bitcast.418, f32[13,13824]{1,0:T(8,128)} %constant.88.clone, s32[]{:T(128)S(6)} %select_n.79), kind=kOutput, calls=%fused_computation.75 | convolution fusion | flops 69009408 | bytes 1892356 | tf_op jit(solution)/shard_map/dot_general | solution.py:340
  103.6 19.8 %shard_map.69 = f32[8,32,128]{2,1,0:T(8,128)} custom-call(f32[8,32,128]{2,1,0:T(8,128)} %bitcast.430), custom_call_target="tpu_custom_call" | custom-call | tf_op jit(solution)/shard_map/pallas_call | solution.py:310
  126.9 3.1 %fusion.135 = f32[2,27,8,1024]{3,2,1,0:T(8,128)S(1)} fusion(f32[216,2,1024]{2,0,1:T(8,128)S(1)} %fusion.44, f32[216]{0:T(256)S(1)} %copy-done.12, pred[2,1024]{1,0:T(4,128)(4,1)S(1)} %get-tuple-element.48, f32[216]{0:T(256)S(1)} %copy-done.10, f32[2,1024]{1,0:T(2,128)S(1)} %get-tuple-element.41, pred[2,1024]{1,0:T(4,128)(4,1)S(1)} %get-tuple-element.49, ...), kind=kLoop, calls=%fused_computation.211 | loop fusion | flops 13271040 | bytes 3655904
  129.9 3.0 %fusion.37 = f32[216,2,1024]{2,0,1:T(8,128)S(1)} fusion(f32[216,2,1024]{2,0,1:T(8,128)S(1)} %fusion.44, f32[2,1024]{1,0:T(2,128)S(1)} %get-tuple-element.41, f32[2,1024]{1,0:T(2,128)S(1)} %get-tuple-element.12, f32[2,1024]{1,0:T(2,128)S(1)} %get-tuple-element.37, f32[2,1024]{1,0:T(2,128)S(1)} %get-tuple-element.46, f32[2,1024]{1,0:T(2,128)S(1)} %fusion.102, ...), kind=kLoop, calls=%fused_computation.49 | loop fusion | flops 13271040 | bytes 3655904 | tf_op jit(solution)/shard_map/jit(_where)/select_n | solution.py:241
  132.9 2.6 %copy.65 = f32[216,2,1024]{2,1,0:T(2,128)} copy(f32[216,2,1024]{2,0,1:T(8,128)S(1)} %fusion.37) | data formatting | bytes 3538944
  135.6 1.7 %fusion.54 = f32[13,2048]{1,0:T(8,128)S(1)} fusion(f32[216,2048]{1,0:T(8,128)S(1)} %bitcast.416, f32[13,13824]{1,0:T(8,128)} %constant.88.clone, s32[]{:T(128)S(6)} %select_n.79), kind=kOutput, calls=%fused_computation.73 | convolution fusion | flops 69009408 | bytes 1892356 | tf_op jit(solution)/shard_map/dot_general | solution.py:340
  138.1 19.8 %shard_map.70 = f32[8,32,128]{2,1,0:T(8,128)} custom-call(f32[8,32,128]{2,1,0:T(8,128)} %bitcast.432), custom_call_target="tpu_custom_call" | custom-call | tf_op jit(solution)/shard_map/pallas_call | solution.py:310
  (83 shorter events, 19.2 us)
Async XLA Ops:
  4.1 26.2 %collective-permute-start = (f32[216,1,1024]{2,0,1:T(8,128)}, f32[216,1,1024]{2,0,1:T(8,128)S(1)}, u32[]{:S(2)}, u32[]{:S(2)}) collective-permute-start(f32[216,1,1024]{2,0,1:T(8,128)} %get-tuple-element.32), channel_id=1, source_target_pairs={{0,1},{1,2},{2,3},{3,4},{4,5},{5,6},{6,7},{8,9},{9,10},{10,11},{11... | collective-permute-start | bytes 2654216 | tf_op jit(solution)/shard_map/ppermute | solution.py:28
  6.0 26.1 %collective-permute-start.1 = (f32[216,1,1024]{2,0,1:T(8,128)}, f32[216,1,1024]{2,0,1:T(8,128)S(1)}, u32[]{:S(2)}, u32[]{:S(2)}) collective-permute-start(f32[216,1,1024]{2,0,1:T(8,128)} %get-tuple-element.33), channel_id=1, source_target_pairs={{1,0},{2,1},{3,2},{4,3},{5,4},{6,5},{7,6},{9,8},{10,9},{11,10},{12... | collective-permute-start | bytes 2654216 | tf_op jit(solution)/shard_map/ppermute | solution.py:30
  16.1 17.0 %copy-start.2 = (f32[1,216]{1,0:T(1,128)}, f32[1,216]{1,0:T(1,128)S(1)}, u32[]{:S(2)}) copy-start(f32[1,216]{1,0:T(1,128)S(1)} %get-tuple-element.36) | copy-start | bytes 2596
  16.1 17.0 %copy-start.5 = (f32[1,216]{1,0:T(1,128)}, f32[1,216]{1,0:T(1,128)S(1)}, u32[]{:S(2)}) copy-start(f32[1,216]{1,0:T(1,128)S(1)} %get-tuple-element.34) | copy-start | bytes 2596
  16.1 17.0 %copy-start.17 = (pred[216]{0:T(512)(128)(4,1)}, pred[216]{0:T(512)(128)(4,1)S(1)}, u32[]{:S(2)}) copy-start(pred[216]{0:T(512)(128)(4,1)S(1)} %get-tuple-element.62) | copy-start | bytes 652
  16.1 17.0 %copy-start.19 = (pred[216]{0:T(512)(128)(4,1)}, pred[216]{0:T(512)(128)(4,1)S(1)}, u32[]{:S(2)}) copy-start(pred[216]{0:T(512)(128)(4,1)S(1)} %get-tuple-element.63) | copy-start | bytes 652
  19.1 14.0 %copy-start.21 = (pred[216]{0:T(512)(128)(4,1)}, pred[216]{0:T(512)(128)(4,1)S(1)}, u32[]{:S(2)}) copy-start(pred[216]{0:T(512)(128)(4,1)S(1)} %broadcast_compare_fusion.5) | copy-start | bytes 652
  19.8 13.3 %copy-start.13 = (pred[1024]{0:T(1024)(128)(4,1)}, pred[1024]{0:T(1024)(128)(4,1)S(1)}, u32[]{:S(2)}) copy-start(pred[1024]{0:T(1024)(128)(4,1)S(1)} %get-tuple-element.60) | copy-start | bytes 3076
  19.8 13.3 %copy-start.15 = (pred[1024]{0:T(1024)(128)(4,1)}, pred[1024]{0:T(1024)(128)(4,1)S(1)}, u32[]{:S(2)}) copy-start(pred[1024]{0:T(1024)(128)(4,1)S(1)} %get-tuple-element.61) | copy-start | bytes 3076
  37.0 30.2 %copy-start.3 = (f32[1,216]{1,0:T(1,128)S(1)}, f32[1,216]{1,0:T(1,128)}, u32[]{:S(2)}) copy-start(f32[1,216]{1,0:T(1,128)} %copy-done.2) | copy-start | bytes 2596
  37.0 30.2 %copy-start.6 = (f32[1,216]{1,0:T(1,128)S(1)}, f32[1,216]{1,0:T(1,128)}, u32[]{:S(2)}) copy-start(f32[1,216]{1,0:T(1,128)} %copy-done.5) | copy-start | bytes 2596
  37.1 30.2 %copy-start.9 = (f32[216]{0:T(256)S(1)}, f32[216]{0:T(256)}, u32[]{:S(2)}) copy-start(f32[216]{0:T(256)} %get-tuple-element.52) | copy-start | bytes 2596
  37.1 30.2 %copy-start.11 = (f32[216]{0:T(256)S(1)}, f32[216]{0:T(256)}, u32[]{:S(2)}) copy-start(f32[216]{0:T(256)} %get-tuple-element.53) | copy-start | bytes 2596
  70.5 25.9 %collective-permute-start.2 = (f32[216,1,1024]{2,0,1:T(8,128)S(1)}, f32[216,1,1024]{2,0,1:T(8,128)S(1)}, u32[]{:S(2)}, u32[]{:S(2)}) collective-permute-start(f32[216,1,1024]{2,0,1:T(8,128)S(1)} %get-tuple-element.26), channel_id=1, source_target_pairs={{0,1},{1,2},{2,3},{3,4},{4,5},{5,6},{6,7},{8,9},{9,10},{10,11},{11... | collective-permute-start | bytes 2654216 | tf_op jit(solution)/shard_map/ppermute | solution.py:28
  72.4 25.8 %collective-permute-start.3 = (f32[216,1,1024]{2,0,1:T(8,128)S(1)}, f32[216,1,1024]{2,0,1:T(8,128)S(1)}, u32[]{:S(2)}, u32[]{:S(2)}) collective-permute-start(f32[216,1,1024]{2,0,1:T(8,128)S(1)} %get-tuple-element.27), channel_id=1, source_target_pairs={{1,0},{2,1},{3,2},{4,3},{5,4},{6,5},{7,6},{9,8},{10,9},{11,10},{12... | collective-permute-start | bytes 2654216 | tf_op jit(solution)/shard_map/ppermute | solution.py:30
  78.9 19.4 %copy-start.4 = (f32[1,216]{1,0:T(1,128)S(1)}, f32[1,216]{1,0:T(1,128)}, u32[]{:S(2)}) copy-start(f32[1,216]{1,0:T(1,128)} %copy-done.2) | copy-start | bytes 2596
  78.9 19.4 %copy-start.7 = (f32[1,216]{1,0:T(1,128)S(1)}, f32[1,216]{1,0:T(1,128)}, u32[]{:S(2)}) copy-start(f32[1,216]{1,0:T(1,128)} %copy-done.5) | copy-start | bytes 2596
  78.9 19.3 %copy-start.14 = (pred[1024]{0:T(1024)(128)(4,1)S(1)}, pred[1024]{0:T(1024)(128)(4,1)}, u32[]{:S(2)}) copy-start(pred[1024]{0:T(1024)(128)(4,1)} %copy-done.13) | copy-start | bytes 3076
  78.9 19.3 %copy-start.16 = (pred[1024]{0:T(1024)(128)(4,1)S(1)}, pred[1024]{0:T(1024)(128)(4,1)}, u32[]{:S(2)}) copy-start(pred[1024]{0:T(1024)(128)(4,1)} %copy-done.15) | copy-start | bytes 3076
  78.9 19.3 %copy-start.18 = (pred[216]{0:T(512)(128)(4,1)S(1)}, pred[216]{0:T(512)(128)(4,1)}, u32[]{:S(2)}) copy-start(pred[216]{0:T(512)(128)(4,1)} %copy-done.17) | copy-start | bytes 652
  78.9 19.3 %copy-start.20 = (pred[216]{0:T(512)(128)(4,1)S(1)}, pred[216]{0:T(512)(128)(4,1)}, u32[]{:S(2)}) copy-start(pred[216]{0:T(512)(128)(4,1)} %copy-done.19) | copy-start | bytes 652
  79.0 19.3 %copy-start.22 = (pred[216]{0:T(512)(128)(4,1)S(1)}, pred[216]{0:T(512)(128)(4,1)}, u32[]{:S(2)}) copy-start(pred[216]{0:T(512)(128)(4,1)} %copy-done.21) | copy-start | bytes 652
  101.1 25.7 %copy-start.10 = (f32[216]{0:T(256)S(1)}, f32[216]{0:T(256)}, u32[]{:S(2)}) copy-start(f32[216]{0:T(256)} %get-tuple-element.52) | copy-start | bytes 2596
  101.1 25.7 %copy-start.12 = (f32[216]{0:T(256)S(1)}, f32[216]{0:T(256)}, u32[]{:S(2)}) copy-start(f32[216]{0:T(256)} %get-tuple-element.53) | copy-start | bytes 2596
  (4 other events, 12.5 us)

commit v2 on v0

v2 whole, which is shorter than its diff:
```python
import functools

import jax
import jax.numpy as jnp
import numpy as np
from jax import lax
from jax.experimental import pallas as pl
from jax.experimental.pallas import tpu as pltpu
from jax.sharding import PartitionSpec as P

QUAD_ABSCISSAE = 24
RUN = 6
STEPS = 2


MOMENTUM_RATIO = 2.0 / 3.0
SHEAR_EXPONENT = 0.81
SHEAR_REFERENCE = 0.05
TIME_INCREMENT = 0.03125

NODES = RUN * RUN * RUN
HALF = NODES // 2
PAIRS = RUN * RUN
ROWS = 32
MESH = pl.DeviceIdType.MESH


def hermite_rule(points):
    start_value = np.pi ** (-0.25)
    node_list = np.zeros(points)
    weight_list = np.zeros(points)
    guess_root = 0.0
    slope_value = 1.0
    for index in range((points + 1) // 2):
        if index == 0:
            guess_root = np.sqrt(2.0 * points + 1.0) - 1.85575 * (2.0 * points + 1.0) ** (-0.16667)
        elif index == 1:
            guess_root = guess_root - 1.14 * points**0.426 / guess_root
        elif index == 2:
            guess_root = 1.86 * guess_root - 0.86 * node_list[0]
        elif index == 3:
            guess_root = 1.91 * guess_root - 0.91 * node_list[1]
        else:
            guess_root = 2.0 * guess_root - node_list[index - 2]
        for sweep in range(60):
            poly_now = start_value
            poly_prev = 0.0
            for degree in range(points):
                poly_old = poly_prev
                poly_prev = poly_now
                poly_now = (
                    guess_root * np.sqrt(2.0 / (degree + 1)) * poly_prev
                    - np.sqrt(degree / (degree + 1.0)) * poly_old
                )
            slope_value = np.sqrt(2.0 * points) * poly_prev
            guess_root = guess_root - poly_now / slope_value
        node_list[index] = guess_root
        node_list[points - 1 - index] = -guess_root
        weight_list[index] = 2.0 / (slope_value * slope_value)
        weight_list[points - 1 - index] = weight_list[index]
    return (node_list[::-1].copy(), weight_list[::-1].copy())


def one_dimensional_tables(points):
    abscissa, weights = hermite_rule(points)
    speed = np.sqrt(2.0) * abscissa
    weight = weights * np.exp(abscissa * abscissa) / np.sqrt(np.pi)
    return np.concatenate([speed, weight, TIME_INCREMENT * np.abs(speed)])


def step_parameters(moment, kind, boundary):
    density = moment[0]
    first = moment[1:4]
    flow = [value / density for value in first]
    trace = moment[4] + moment[5] + moment[6]
    square = flow[0] * flow[0] + flow[1] * flow[1] + flow[2] * flow[2]
    temperature = (trace / density - square) / 3.0
    along = flow[0] * first[0] + flow[1] * first[1] + flow[2] * first[2]
    pairs = ((4, 7, 8), (7, 5, 9), (8, 9, 6))
    heat = []
    for d in range(3):
        tensor = (
            moment[pairs[d][0]] * flow[0]
            + moment[pairs[d][1]] * flow[1]
            + moment[pairs[d][2]] * flow[2]
        )
        heat.append(
            0.5
            * (
                moment[10 + d]
                - 2.0 * tensor
                + square * first[d]
                - flow[d] * trace
                + 2.0 * flow[d] * along
                - flow[d] * square * density
            )
        )
    pressure = density * temperature
    rate = (
        TIME_INCREMENT
        * pressure
        / (SHEAR_REFERENCE * jnp.exp(SHEAR_EXPONENT * jnp.log(temperature)))
    )
    keep = 1.0 / (1.0 + rate)
    scale = (1.0 - MOMENTUM_RATIO) / (5.0 * pressure * temperature)

    def pick(fluid, wall, inlet, outlet):
        return jnp.where(
            kind == 0, fluid, jnp.where(kind == 1, wall, jnp.where(kind == 2, inlet, outlet))
        )

    level = pick(temperature, boundary[5], boundary[4], 1.0)
    amount = pick(density * rate * keep, density, boundary[0], 0.0)
    return (
        [pick(keep, 0.0, 0.0, 1.0), amount / (level * jnp.sqrt(level))]
        + [pick(flow[d], 0.0, boundary[1 + d], 0.0) for d in range(3)]
        + [0.5 / level]
        + [pick(heat[d] * scale, 0.0, 0.0, 0.0) for d in range(3)]
        + [density, first[0], first[1], first[2], trace]
    )


def added_moments(power, amount, flow, inverse, heat):
    planes = {}

    def product(i, j, k):
        if (i, j) not in planes:
            planes[i, j] = power[0][i] * power[1][j]
        return planes[i, j] * power[2][k]

    def shifted(base, d, n=1):
        return tuple(base[e] + (n if e == d else 0) for e in range(3))

    def squared(base):
        return product(*shifted(base, 0, 2)) + product(*shifted(base, 1, 2)) + product(*shifted(base, 2, 2))

    double = inverse + inverse

    def whole(base):
        total = product(*base)
        for d in range(3):
            with_d = shifted(base, d)
            total = total + heat[d] * (double * squared(with_d) - 5.0 * product(*with_d))
        return total

    def with_heat(base, d):
        at = shifted(base, d)
        fourth = None
        for e in range(3):
            for f in range(3):
                term = product(*shifted(shifted(at, e, 2), f, 2))
                fourth = term if fourth is None else fourth + term
        return heat[d] * (double * fourth - 5.0 * squared(at))

    zero = (0, 0, 0)
    none = amount * whole(zero)
    one = [amount * whole(shifted(zero, d)) for d in range(3)]
    two = squared(zero)
    for d in range(3):
        two = two + with_heat(zero, d)
    two = amount * two
    square = flow[0] * flow[0] + flow[1] * flow[1] + flow[2] * flow[2]
    momentum = [one[d] + flow[d] * none for d in range(3)]
    trace = (
        two
        + 2.0 * (flow[0] * one[0] + flow[1] * one[1] + flow[2] * one[2])
        + square * none
    )
    return [none] + momentum + [trace]


def kernel(
    groups,
    digits,
    cells,
    state_ref,
    kind_ref,
    boundary_ref,
    table_ref,
    out_ref,
    macro_ref,
    raw,
    h_first,
    h_second,
    moved,
    halo,
    acc,
    edge,
    got_edge,
    part,
    got_a,
    mine,
    got_b,
    gathered,
    gauss,
    bend,
    tilt,
    keep_ref,
    input_sem,
    send_sem,
    recv_sem,
    edge_send,
    edge_recv,
    halo_send,
    halo_recv,
):
    points = RUN * digits
    vel = lax.axis_index("vel")
    cell = lax.axis_index("cell")
    jc = lax.rem(vel, digits)
    jb = lax.rem(vel // digits, digits)
    ja = vel // (digits * digits)
    lo = lax.rem(vel, 2)
    row = lax.rem(vel // 2, 8)
    col = vel // 16
    here = col * 2 + lo
    up = lax.rem(cell + 1, cells)
    down = lax.rem(cell + cells - 1, cells)

    def peer_a(other):
        return ((other // 2) * 16 + row * 2 + lax.rem(other, 2), cell)

    def peer_b(other):
        return (col * 16 + other * 2 + lo, cell)

    load = pltpu.make_async_copy(state_ref, raw, input_sem)
    load.start()
    barrier = pltpu.get_barrier_semaphore()
    for other in (up, down):
        pl.semaphore_signal(barrier, inc=1, device_id=(vel, other), device_id_type=MESH)
    if groups:
        for k in range(1, 8):
            pl.semaphore_signal(
                barrier, inc=1, device_id=peer_a(lax.rem(here + k, 8)), device_id_type=MESH
            )
            pl.semaphore_signal(
                barrier, inc=1, device_id=peer_b(lax.rem(row + k, 8)), device_id_type=MESH
            )
    pl.semaphore_wait(barrier, 16 if groups else 2)

    lane = lax.broadcasted_iota(jnp.int32, (8, 128), 1)
    sub = lax.broadcasted_iota(jnp.int32, (8, 128), 0)
    in_z = lax.rem(lane, 32)
    z_first, z_last = in_z == 0, in_z == 31
    y_low, y_high = lane < 32, lane >= 96
    y_first, y_last = sub == 0, sub == 7
    has_down = jnp.where(cell > 0, 1.0, 0.0).astype(jnp.float32)
    has_up = jnp.where(cell < cells - 1, 1.0, 0.0).astype(jnp.float32)

    def speed(m, digit):
        return table_ref[4 * m + digit] if digits == 4 else table_ref[m]

    def weight(m, digit):
        return table_ref[points + 4 * m + digit] if digits == 4 else table_ref[points + m]

    def courant(m, digit):
        return table_ref[2 * points + 4 * m + digit] if digits == 4 else table_ref[2 * points + m]

    def run_sums(values):
        sums = None
        for mc, value in enumerate(values):
            sz = speed(mc, jc)
            terms = [weight(mc, jc) * value]
            for _ in range(3):
                terms.append(sz * terms[-1])
            sums = terms if sums is None else [x + y for x, y in zip(sums, terms)]
        return sums

    def add_moments(ref, place, sums, ma, mb, factor):
        sx, sy = speed(ma, ja), speed(mb, jb)
        w = weight(ma, ja) * weight(mb, jb) * factor
        wx, wy = w * sx, w * sy
        t0, t1, t2, t3 = sums
        plane_square = sx * sx + sy * sy
        both = plane_square * t0 + t2
        rows = [
            w * t0,
            wx * t0,
            wy * t0,
            w * t1,
            (wx * sx) * t0,
            (wy * sy) * t0,
            w * t2,
            (wx * sy) * t0,
            wx * t1,
            wy * t1,
            wx * both,
            wy * both,
            w * (plane_square * t1 + t3),
        ]
        for r in range(13):
            ref[r, place] += rows[r]

    def shift_y(value, positive):
        turned = pltpu.roll(value, 32 if positive else 96, 1)
        carried = pltpu.roll(turned, 1 if positive else 7, 0)
        edge_rows, lanes = (y_first, y_low) if positive else (y_last, y_high)
        return jnp.where(lanes, jnp.where(edge_rows, 0.0, carried), turned)

    def shift_z(value, positive):
        turned = pltpu.roll(value, 1 if positive else 127, 1)
        return jnp.where(z_first if positive else z_last, 0.0, turned)

    def relaxed(i, ma, mb, plane, pi, outer):
        base = gauss[ma, plane] * gauss[RUN + mb, plane]
        bend_xy = bend[ma, plane] + bend[RUN + mb, plane]
        tilt_xy = tilt[ma, plane] + tilt[RUN + mb, plane]
        keep = keep_ref[plane]
        values = []
        if outer:
            kx = courant(ma, ja) * jnp.where(pi == 1, has_down, has_up)
        for mc in range(RUN):
            node = i * RUN + mc
            value = moved[plane, node]
            if outer:
                value = value + kx * halo[outer - 1, pi, node - pi * HALF]
            t = (tilt_xy + tilt[2 * RUN + mc, plane]) * (bend_xy + bend[2 * RUN + mc, plane])
            values.append(keep * value + (base * gauss[2 * RUN + mc, plane]) * (1.0 + t))
        return values

    def new_plane(step, i, ma, mb, plane, pi, outer):
        if step == 0:
            return [
                raw[pl.ds((i * RUN + mc) * 16 + plane, 8, stride=2), :] for mc in range(RUN)
            ]
        return relaxed(i, ma, mb, plane, pi, step if outer else 0)

    def send_edges(step, held):
        copies = []
        for pi, other in ((1, up), (0, down)):
            copies.append(
                pltpu.make_async_remote_copy(
                    src_ref=edge.at[step, pi],
                    dst_ref=got_edge.at[step, pi],
                    send_sem=edge_send.at[step, pi],
                    recv_sem=edge_recv.at[step, pi],
                    device_id=(vel, other),
                    device_id_type=MESH,
                )
            )
        for pi, other in ((1, up), (0, down)):
            copies.append(
                pltpu.make_async_remote_copy(
                    src_ref=held.at[pi, pl.ds(pi * HALF, HALF)],
                    dst_ref=halo.at[step, pi],
                    send_sem=halo_send.at[step, pi],
                    recv_sem=halo_recv.at[step, pi],
                    device_id=(vel, other),
                    device_id_type=MESH,
                )
            )
        for copy in copies:
            copy.start()
        return copies[:2], copies[2:]

    def exchange(step, phase, source, target, index, peer):
        copies = []
        for k in range(1, 8):
            other = lax.rem(index + k, 8)
            copy = pltpu.make_async_remote_copy(
                src_ref=source(other),
                dst_ref=target,
                send_sem=send_sem.at[step, phase, k - 1],
                recv_sem=recv_sem.at[step, phase, k - 1],
                device_id=peer(other),
                device_id_type=MESH,
            )
            copy.start()
            copies.append(copy)
        return copies

    def slice_rows(index):
        return pl.ds(pl.multiple_of(index * ROWS, ROWS), ROWS)

    def parameters_of(step, index, total_ref):
        moment = [total_ref[pl.ds(2 * r, 2), :] for r in range(13)]
        kind = kind_ref[pl.ds(2 * index, 2), :]
        boundary = [boundary_ref[r] for r in range(6)]
        rows = step_parameters(moment, kind, boundary)
        for r in range(ROWS // 2):
            value = rows[r] if r < len(rows) else jnp.zeros((2, 128), jnp.float32)
            gathered[step, pl.ds(index * ROWS + 2 * r, 2), :] = value

    def all_sums(step):
        for r in range(ROWS // 2):
            for p in range(2):
                value = acc[r, p] if r < 13 else jnp.zeros((8, 128), jnp.float32)
                if r < 13:
                    mask = has_down if p == 0 else has_up
                    value = value + mask * got_edge[step, 1 - p, r]
                part[step, pl.ds(2 * r + p, 8, stride=ROWS), :] = value
        if not groups:
            for index in range(8):
                mine[step] = part[step, pl.ds(index * ROWS, ROWS), :]
                parameters_of(step, index, mine.at[step])
            return
        copies = exchange(
            step, 0, lambda other: part.at[step, slice_rows(other)], got_a.at[step, here], here, peer_a
        )
        got_a[step, here] = part[step, slice_rows(here), :]
        for copy in copies:
            copy.wait()
        total = got_a[step, 0]
        for k in range(1, 8):
            total = total + got_a[step, k]
        mine[step] = total
        copies = exchange(
            step, 1, lambda other: mine.at[step], got_b.at[step, row], row, peer_b
        )
        got_b[step, row] = total
        for copy in copies:
            copy.wait()
        total = got_b[step, 0]
        for k in range(1, 8):
            total = total + got_b[step, k]
        acc_rows = got_b.at[step, row]
        acc_rows[...] = total
        parameters_of(step, here, acc_rows)
        block = gathered.at[step, slice_rows(here)]
        copies = exchange(step, 2, lambda other: block, block, here, peer_a)
        for copy in copies:
            copy.wait()

    def gathered_rows(step, r):
        return [gathered[step, pl.ds(2 * r + p, 8, stride=ROWS), :] for p in range(2)]

    def build_tables(step):
        keep, amount, *rest = [gathered_rows(step, r) for r in range(9)]
        for p in range(2):
            keep_ref[p] = keep[p]

        def fill(m, carry):
            for d, digit in enumerate((ja, jb, jc)):
                s = speed(m, digit)
                for p in range(2):
                    c = s - rest[d][p]
                    inverse = rest[3][p]
                    scaled = c * c * inverse
                    value = jnp.exp(-scaled)
                    lift = scaled + scaled
                    if d == 0:
                        value = value * amount[p]
                        lift = lift - 5.0
                    gauss[d * RUN + m, p] = value
                    bend[d * RUN + m, p] = lift
                    tilt[d * RUN + m, p] = c * rest[4 + d][p]
            return carry

        lax.fori_loop(0, RUN, fill, 0)

    load.wait()
    for step in range(STEPS):
        held = h_first if step == 0 else h_second
        edge[step] = jnp.zeros(edge.shape[1:], jnp.float32)
        acc[...] = jnp.zeros(acc.shape, jnp.float32)

        def inner(i, carry, step=step, held=held):
            ma, mb = i // RUN, lax.rem(i, RUN)
            pi = ma // (RUN // 2)
            values = new_plane(step, i, ma, mb, pi, pi, False)
            for mc in range(RUN):
                held[pi, i * RUN + mc] = values[mc]
            add_moments(edge.at[step, pi], slice(None), run_sums(values), ma, mb, courant(ma, ja))
            return carry

        lax.fori_loop(0, PAIRS, inner, 0)
        edges, halos = send_edges(step, held)
        if step > 0:
            for copy in halos_before:
                copy.wait()

        def outer(i, carry, step=step, held=held):
            ma, mb = i // RUN, lax.rem(i, RUN)
            pi = ma // (RUN // 2)
            values = new_plane(step, i, ma, mb, 1 - pi, pi, True)
            for mc in range(RUN):
                held[1 - pi, i * RUN + mc] = values[mc]
            return carry

        lax.fori_loop(0, PAIRS, outer, 0)

        for half in range(2):

            def transport(j, carry, half=half, held=held):
                ma = j // (RUN // 2)
                mb = half * (RUN // 2) + lax.rem(j, RUN // 2)
                pi = ma // (RUN // 2)
                i = ma * RUN + mb
                kx, ky = courant(ma, ja), courant(mb, jb)
                at_inner, at_outer = [], []
                for mc in range(RUN):
                    node = i * RUN + mc
                    kz = courant(mc, jc)
                    stay = 1.0 - (kx + ky + kz)
                    near, far = held[pi, node], held[1 - pi, node]

                    def flat(value):
                        return (
                            stay * value
                            + ky * shift_y(value, half == 1)
                            + kz * shift_z(value, mc >= RUN // 2)
                        )

                    at_inner.append(flat(near) + kx * far)
                    at_outer.append(flat(far))
                    moved[pi, node] = at_inner[-1]
                    moved[1 - pi, node] = at_outer[-1]
                add_moments(acc, pi, run_sums(at_inner), ma, mb, 1.0)
                add_moments(acc, 1 - pi, run_sums(at_outer), ma, mb, 1.0)
                return carry

            lax.fori_loop(0, PAIRS // 2, transport, 0)
        for copy in edges:
            copy.wait()
        all_sums(step)
        build_tables(step)
        halos_before = halos

    for copy in halos_before:
        copy.wait()

    def last(i, carry):
        ma, mb = i // RUN, lax.rem(i, RUN)
        pi = ma // (RUN // 2)
        for plane, is_outer in ((pi, 0), (1 - pi, STEPS)):
            values = relaxed(i, ma, mb, plane, pi, is_outer)
            for mc in range(RUN):
                out_ref[pl.ds((i * RUN + mc) * 16 + plane, 8, stride=2), :] = values[mc]
        return carry

    lax.fori_loop(0, PAIRS, last, 0)

    final = STEPS - 1
    for p in range(2):
        keep, amount, ux, uy, uz, inverse, qx, qy, qz, *old = [
            gathered_rows(final, r)[p] for r in range(14)
        ]
        flow, heat = (ux, uy, uz), (qx, qy, qz)

        def sums(a, carry):
            s, w = table_ref[a], table_ref[points + a]
            result = []
            for d in range(3):
                c = s - flow[d]
                term = w * jnp.exp(-(c * c * inverse))
                for n in range(6):
                    result.append(carry[d * 6 + n] + term)
                    term = term * c
            return tuple(result)

        power = lax.fori_loop(
            0, points, sums, tuple(jnp.zeros((8, 128), jnp.float32) for _ in range(18))
        )
        power = [power[d * 6 : d * 6 + 6] for d in range(3)]
        added = added_moments(power, amount, flow, inverse, heat)
        density, mx, my, mz, trace = [keep * x + y for x, y in zip(old, added)]
        u = [mx / density, my / density, mz / density]
        square = u[0] * u[0] + u[1] * u[1] + u[2] * u[2]
        result = [density] + u + [(trace / density - square) / 3.0]
        for r in range(5):
            macro_ref[pl.ds(r * 16 + p, 8, stride=2), :] = result[r]


def interleaved(array):
    lead = array.shape[:-2]
    return array.reshape(lead + (2, 8, 128)).swapaxes(-3, -2).reshape(-1, 128)


def restored(array, lead):
    return array.reshape((lead, 8, 2, 128)).swapaxes(1, 2).reshape(lead, 2, 1024)


def shards(groups, digits, cells, state_init, cell_kind, boundary_state):
    vmem = functools.partial(pl.BlockSpec, memory_space=pltpu.VMEM)
    smem = functools.partial(pl.BlockSpec, memory_space=pltpu.SMEM)
    table = jnp.asarray(one_dimensional_tables(RUN * digits), jnp.float32)
    f32 = jnp.float32
    state, macro = pl.pallas_call(
        functools.partial(kernel, groups, digits, cells),
        out_shape=(
            jax.ShapeDtypeStruct((NODES * 16, 128), f32),
            jax.ShapeDtypeStruct((80, 128), f32),
        ),
        in_specs=[pl.BlockSpec(memory_space=pl.ANY), vmem(), smem(), smem()],
        out_specs=(vmem(), vmem()),
        scratch_shapes=[
            pltpu.VMEM((NODES * 16, 128), f32),
            pltpu.VMEM((2, NODES, 8, 128), f32),
            pltpu.VMEM((2, NODES, 8, 128), f32),
            pltpu.VMEM((2, NODES, 8, 128), f32),
            pltpu.VMEM((STEPS, 2, HALF, 8, 128), f32),
            pltpu.VMEM((13, 2, 8, 128), f32),
            pltpu.VMEM((STEPS, 2, 13, 8, 128), f32),
            pltpu.VMEM((STEPS, 2, 13, 8, 128), f32),
            pltpu.VMEM((STEPS, 8 * ROWS, 128), f32),
            pltpu.VMEM((STEPS, 8, ROWS, 128), f32),
            pltpu.VMEM((STEPS, ROWS, 128), f32),
            pltpu.VMEM((STEPS, 8, ROWS, 128), f32),
            pltpu.VMEM((STEPS, 8 * ROWS, 128), f32),
            pltpu.VMEM((3 * RUN, 2, 8, 128), f32),
            pltpu.VMEM((3 * RUN, 2, 8, 128), f32),
            pltpu.VMEM((3 * RUN, 2, 8, 128), f32),
            pltpu.VMEM((2, 8, 128), f32),
            pltpu.SemaphoreType.DMA,
            pltpu.SemaphoreType.DMA((STEPS, 3, 7)),
            pltpu.SemaphoreType.DMA((STEPS, 3, 7)),
            pltpu.SemaphoreType.DMA((STEPS, 2)),
            pltpu.SemaphoreType.DMA((STEPS, 2)),
            pltpu.SemaphoreType.DMA((STEPS, 2)),
            pltpu.SemaphoreType.DMA((STEPS, 2)),
        ],
        compiler_params=pltpu.CompilerParams(
            collective_id=0, has_side_effects=True, vmem_limit_bytes=40 * 1024 * 1024
        ),
    )(interleaved(state_init), interleaved(cell_kind), boundary_state, table)
    return restored(state, NODES), restored(macro, 5)


def solution(mesh):
    in_specs = (P("vel", "cell", None), P("cell", None), P())
    out_specs = (P("vel", "cell", None), P(None, "cell", None))
    body = functools.partial(shards, True, 4, 8)
    return jax.shard_map(body, mesh=mesh, in_specs=in_specs, out_specs=out_specs, check_vma=False)
```

time: 1710 us -> 74.6 us (0.04); the launches traced: 1680 us -> 73.6 us
  waiting for transfers between devices: 1570 us -> 0 us
  Pallas kernels: 0 us -> 67.7 us
  starting transfers between devices: 47.6 us -> 0 us
  other arithmetic: 28.5 us -> 0 us
    psum x3 -> x0, waiting for transfers between devices: 1530 us -> none  [cell_fields(): moment_quantities = equilibrium_fields(lax.psum(moments, 'vel'))]
    pallas_call x0 -> x1, Pallas kernels: none -> 67.7 us  [shards(): pl.pallas_call(functools.partial(kernel, groups, digits, cells), out_shap...]
    ppermute x4 -> x0, starting transfers between devices: 47.5 us -> none  [the longest x2 42.5 us: extended(): lax.ppermute(tail, axis, [(i, (i + 1) % count) for i in range(ends)])]
    ppermute x4 -> x0, waiting for transfers between devices: 35.8 us -> none  [the longest x2 29.3 us: extended(): lax.ppermute(head, axis, [((i + 1) % count, i) for i in range(ends)])]
  transfers between devices with their start and end apart: 7 -> 0, of which waited for: 6 -> 0; matrix products, arithmetic and copies ran while one was open for 1% -> 0% of each run, Pallas kernels for 0% -> 0%
where the time goes in v2:
time: 74.6 us; the launch traced here: 73.6 us
  Pallas kernels  67.7 us (91%)
  local copies, waits for them, and re-layouts  5.3 us (7%)
    pallas_call x1, Pallas kernels, shards(): pl.pallas_call(functools.partial(kernel, groups, digits, cells), out_shap...  67.7 us
    unnamed x10, local copies, waits for them, and re-layouts  5.3 us

profile of v2, /device:TPU:1, one launch (start us, length us, event | category | flops | bytes accessed | tf_op | source)
XLA Modules:
  0.0 73.6 jit_solution(16648090250766180791)
XLA Ops:
  0.6 0.0 copy-start
  0.6 1.5 %copy-done = f32[216,2,1024]{2,1,0:T(2,128)S(1)} copy-done((f32[216,2,1024]{2,1,0:T(2,128)S(1)}, f32[216,2,1024]{2,1,0:T(2,128)}, u32[]{:S(2)}) %copy-start) | copy-done | bytes 1769496
  2.1 0.0 copy-start.1
  2.1 0.7 copy-done.1
  2.8 0.0 copy-start.2
  2.8 0.7 copy-done.2
  3.5 0.0 copy-start.3
  3.5 0.7 copy-done.3
  4.1 67.7 %shard_map.59 = (f32[3456,128]{1,0:T(8,128)S(1)}, f32[80,128]{1,0:T(8,128)S(1)}) custom-call(f32[3456,128]{1,0:T(8,128)S(1)} %bitcast.21, s32[16,128]{1,0:T(8,128)S(1)} %bitcast.23, f32[6]{0:T(128)S(1)} %copy-done.2, f32[72]{0:T(128)S(1)} %copy-done.3), custom_call_target="tpu_custom_call" | custom-call | tf_op jit(solution)/shard_map/pallas_call | solution.py:578
  71.8 1.2 %copy.12 = f32[216,2,1024]{2,1,0:T(2,128)} copy(f32[216,2,1024]{2,1,0:T(2,128)S(1)} %bitcast.20) | data formatting | bytes 3538944
  73.0 0.6 copy.13
Async XLA Ops:
  0.6 1.5 %copy-start = (f32[216,2,1024]{2,1,0:T(2,128)S(1)}, f32[216,2,1024]{2,1,0:T(2,128)}, u32[]{:S(2)}) copy-start(f32[216,2,1024]{2,1,0:T(2,128)} %param.4) | copy-start | bytes 5308420
  2.1 0.7 copy-start.1
  2.8 0.7 copy-start.2
  3.5 0.7 copy-start.3

commit v3 on v2

--- a/solution.py
+++ b/solution.py
@@ -21,6 +21,7 @@
 NODES = RUN * RUN * RUN
 HALF = NODES // 2
 PAIRS = RUN * RUN
+USED = 26
 ROWS = 32
 MESH = pl.DeviceIdType.MESH
 
@@ -174,11 +175,12 @@
     digits,
     cells,
     state_ref,
-    kind_ref,
+    kind_hbm,
     boundary_ref,
-    table_ref,
     out_ref,
     macro_ref,
+    kind_ref,
+    table_ref,
     raw,
     h_first,
     h_second,
@@ -213,18 +215,21 @@
     lo = lax.rem(vel, 2)
     row = lax.rem(vel // 2, 8)
     col = vel // 16
-    here = col * 2 + lo
+    here = col * 2 + lax.rem(row, 2)
+    there = (row // 2) * 2 + lo
     up = lax.rem(cell + 1, cells)
     down = lax.rem(cell + cells - 1, cells)
 
     def peer_a(other):
-        return ((other // 2) * 16 + row * 2 + lax.rem(other, 2), cell)
+        return ((other // 2) * 16 + (row // 2 * 2 + lax.rem(other, 2)) * 2 + lo, cell)
 
     def peer_b(other):
-        return (col * 16 + other * 2 + lo, cell)
-
-    load = pltpu.make_async_copy(state_ref, raw, input_sem)
-    load.start()
+        return (col * 16 + (other // 2 * 2 + lax.rem(row, 2)) * 2 + lax.rem(other, 2), cell)
+
+    loads = [
+        pltpu.make_async_copy(state_ref, raw, input_sem.at[0]),
+        pltpu.make_async_copy(kind_hbm, kind_ref, input_sem.at[1]),
+    ]
     barrier = pltpu.get_barrier_semaphore()
     for other in (up, down):
         pl.semaphore_signal(barrier, inc=1, device_id=(vel, other), device_id_type=MESH)
@@ -234,9 +239,12 @@
                 barrier, inc=1, device_id=peer_a(lax.rem(here + k, 8)), device_id_type=MESH
             )
             pl.semaphore_signal(
-                barrier, inc=1, device_id=peer_b(lax.rem(row + k, 8)), device_id_type=MESH
+                barrier, inc=1, device_id=peer_b(lax.rem(there + k, 8)), device_id_type=MESH
             )
-    pl.semaphore_wait(barrier, 16 if groups else 2)
+    for copy in loads:
+        copy.start()
+    for index, value in enumerate(one_dimensional_tables(points)):
+        table_ref[index] = jnp.float32(value)
 
     lane = lax.broadcasted_iota(jnp.int32, (8, 128), 1)
     sub = lax.broadcasted_iota(jnp.int32, (8, 128), 0)
@@ -355,7 +363,7 @@
 
     def exchange(step, phase, source, target, index, peer):
         copies = []
-        for k in range(1, 8):
+        for k in (4, 3, 5, 2, 6, 1, 7):
             other = lax.rem(index + k, 8)
             copy = pltpu.make_async_remote_copy(
                 src_ref=source(other),
@@ -369,35 +377,32 @@
             copies.append(copy)
         return copies
 
-    def slice_rows(index):
-        return pl.ds(pl.multiple_of(index * ROWS, ROWS), ROWS)
+    def slice_rows(index, count):
+        return pl.ds(pl.multiple_of(index * ROWS, ROWS), count)
 
     def parameters_of(step, index, total_ref):
         moment = [total_ref[pl.ds(2 * r, 2), :] for r in range(13)]
         kind = kind_ref[pl.ds(2 * index, 2), :]
         boundary = [boundary_ref[r] for r in range(6)]
         rows = step_parameters(moment, kind, boundary)
-        for r in range(ROWS // 2):
-            value = rows[r] if r < len(rows) else jnp.zeros((2, 128), jnp.float32)
-            gathered[step, pl.ds(index * ROWS + 2 * r, 2), :] = value
+        for r in range(9 if step < STEPS - 1 else 14):
+            gathered[step, pl.ds(index * ROWS + 2 * r, 2), :] = rows[r]
 
     def all_sums(step):
-        for r in range(ROWS // 2):
+        for r in range(13):
             for p in range(2):
-                value = acc[r, p] if r < 13 else jnp.zeros((8, 128), jnp.float32)
-                if r < 13:
-                    mask = has_down if p == 0 else has_up
-                    value = value + mask * got_edge[step, 1 - p, r]
+                mask = has_down if p == 0 else has_up
+                value = acc[r, p] + mask * got_edge[step, 1 - p, r]
                 part[step, pl.ds(2 * r + p, 8, stride=ROWS), :] = value
         if not groups:
             for index in range(8):
-                mine[step] = part[step, pl.ds(index * ROWS, ROWS), :]
+                mine[step] = part[step, pl.ds(index * ROWS, USED), :]
                 parameters_of(step, index, mine.at[step])
             return
         copies = exchange(
-            step, 0, lambda other: part.at[step, slice_rows(other)], got_a.at[step, here], here, peer_a
+            step, 0, lambda other: part.at[step, slice_rows(other, USED)], got_a.at[step, here], here, peer_a
         )
-        got_a[step, here] = part[step, slice_rows(here), :]
+        got_a[step, here] = part[step, slice_rows(here, USED), :]
         for copy in copies:
             copy.wait()
         total = got_a[step, 0]
@@ -405,18 +410,18 @@
             total = total + got_a[step, k]
         mine[step] = total
         copies = exchange(
-            step, 1, lambda other: mine.at[step], got_b.at[step, row], row, peer_b
+            step, 1, lambda other: mine.at[step], got_b.at[step, there], there, peer_b
         )
-        got_b[step, row] = total
+        got_b[step, there] = total
         for copy in copies:
             copy.wait()
         total = got_b[step, 0]
         for k in range(1, 8):
             total = total + got_b[step, k]
-        acc_rows = got_b.at[step, row]
+        acc_rows = got_b.at[step, there]
         acc_rows[...] = total
         parameters_of(step, here, acc_rows)
-        block = gathered.at[step, slice_rows(here)]
+        block = gathered.at[step, slice_rows(here, 18 if step < STEPS - 1 else 28)]
         copies = exchange(step, 2, lambda other: block, block, here, peer_a)
         for copy in copies:
             copy.wait()
@@ -448,7 +453,8 @@
 
         lax.fori_loop(0, RUN, fill, 0)
 
-    load.wait()
+    for copy in loads:
+        copy.wait()
     for step in range(STEPS):
         held = h_first if step == 0 else h_second
         edge[step] = jnp.zeros(edge.shape[1:], jnp.float32)
@@ -463,7 +469,9 @@
             add_moments(edge.at[step, pi], slice(None), run_sums(values), ma, mb, courant(ma, ja))
             return carry
 
-        lax.fori_loop(0, PAIRS, inner, 0)
+        lax.fori_loop(0, PAIRS, inner, 0, unroll=3)
+        if step == 0:
+            pl.semaphore_wait(barrier, 16 if groups else 2)
         edges, halos = send_edges(step, held)
         if step > 0:
             for copy in halos_before:
@@ -477,7 +485,7 @@
                 held[1 - pi, i * RUN + mc] = values[mc]
             return carry
 
-        lax.fori_loop(0, PAIRS, outer, 0)
+        lax.fori_loop(0, PAIRS, outer, 0, unroll=3)
 
         for half in range(2):
 
@@ -509,7 +517,7 @@
                 add_moments(acc, 1 - pi, run_sums(at_outer), ma, mb, 1.0)
                 return carry
 
-            lax.fori_loop(0, PAIRS // 2, transport, 0)
+            lax.fori_loop(0, PAIRS // 2, transport, 0, unroll=3)
         for copy in edges:
             copy.wait()
         all_sums(step)
@@ -573,7 +581,6 @@
 def shards(groups, digits, cells, state_init, cell_kind, boundary_state):
     vmem = functools.partial(pl.BlockSpec, memory_space=pltpu.VMEM)
     smem = functools.partial(pl.BlockSpec, memory_space=pltpu.SMEM)
-    table = jnp.asarray(one_dimensional_tables(RUN * digits), jnp.float32)
     f32 = jnp.float32
     state, macro = pl.pallas_call(
         functools.partial(kernel, groups, digits, cells),
@@ -581,9 +588,11 @@
             jax.ShapeDtypeStruct((NODES * 16, 128), f32),
             jax.ShapeDtypeStruct((80, 128), f32),
         ),
-        in_specs=[pl.BlockSpec(memory_space=pl.ANY), vmem(), smem(), smem()],
+        in_specs=[pl.BlockSpec(memory_space=pltpu.HBM), pl.BlockSpec(memory_space=pltpu.HBM), smem()],
         out_specs=(vmem(), vmem()),
         scratch_shapes=[
+            pltpu.VMEM((16, 128), jnp.int32),
+            pltpu.SMEM((3 * RUN * digits,), f32),
             pltpu.VMEM((NODES * 16, 128), f32),
             pltpu.VMEM((2, NODES, 8, 128), f32),
             pltpu.VMEM((2, NODES, 8, 128), f32),
@@ -593,15 +602,15 @@
             pltpu.VMEM((STEPS, 2, 13, 8, 128), f32),
             pltpu.VMEM((STEPS, 2, 13, 8, 128), f32),
             pltpu.VMEM((STEPS, 8 * ROWS, 128), f32),
-            pltpu.VMEM((STEPS, 8, ROWS, 128), f32),
-            pltpu.VMEM((STEPS, ROWS, 128), f32),
-            pltpu.VMEM((STEPS, 8, ROWS, 128), f32),
+            pltpu.VMEM((STEPS, 8, USED, 128), f32),
+            pltpu.VMEM((STEPS, USED, 128), f32),
+            pltpu.VMEM((STEPS, 8, USED, 128), f32),
             pltpu.VMEM((STEPS, 8 * ROWS, 128), f32),
             pltpu.VMEM((3 * RUN, 2, 8, 128), f32),
             pltpu.VMEM((3 * RUN, 2, 8, 128), f32),
             pltpu.VMEM((3 * RUN, 2, 8, 128), f32),
             pltpu.VMEM((2, 8, 128), f32),
-            pltpu.SemaphoreType.DMA,
+            pltpu.SemaphoreType.DMA((2,)),
             pltpu.SemaphoreType.DMA((STEPS, 3, 7)),
             pltpu.SemaphoreType.DMA((STEPS, 3, 7)),
             pltpu.SemaphoreType.DMA((STEPS, 2)),
@@ -612,7 +621,7 @@
         compiler_params=pltpu.CompilerParams(
             collective_id=0, has_side_effects=True, vmem_limit_bytes=40 * 1024 * 1024
         ),
-    )(interleaved(state_init), interleaved(cell_kind), boundary_state, table)
+    )(interleaved(state_init), interleaved(cell_kind), boundary_state)
     return restored(state, NODES), restored(macro, 5)
 
 

time: 74.6 us -> 64.1 us (0.86)
  Pallas kernels: 67.7 us -> 58.1 us
    pallas_call x1, Pallas kernels: 67.7 us -> 58.1 us  [shards(): pl.pallas_call(functools.partial(kernel, groups, digits, cells), out_shap...]
    unnamed x10 -> x8, local copies, waits for them, and re-layouts: 5.3 us -> 4.65 us
where the time goes in v3:
time: 64.1 us; the launch traced here: 63.4 us
  Pallas kernels  58.1 us (91%)
  local copies, waits for them, and re-layouts  4.65 us (7%)
  between operations  0.65 us (1%)
    pallas_call x1, Pallas kernels, shards(): pl.pallas_call(functools.partial(kernel, groups, digits, cells), out_shap...  58.1 us
    unnamed x8, local copies, waits for them, and re-layouts  4.65 us

profile of v3, /device:TPU:1, one launch (start us, length us, event | category | flops | bytes accessed | tf_op | source)
XLA Modules:
  0.0 63.4 jit_solution(5627587844437260952)
XLA Ops:
  0.6 0.0 copy-start
  0.6 1.5 %copy-done = f32[216,2,1024]{2,1,0:T(2,128)S(1)} copy-done((f32[216,2,1024]{2,1,0:T(2,128)S(1)}, f32[216,2,1024]{2,1,0:T(2,128)}, u32[]{:S(2)}) %copy-start) | copy-done | bytes 1769496
  2.1 0.0 copy-start.1
  2.1 0.7 %copy-done.1 = s32[2,1024]{1,0:T(2,128)S(1)} copy-done((s32[2,1024]{1,0:T(2,128)S(1)}, s32[2,1024]{1,0:T(2,128)}, u32[]{:S(2)}) %copy-start.1) | copy-done | bytes 8216
  2.8 0.0 copy-start.2
  2.8 0.7 %copy-done.2 = f32[6]{0:T(128)S(1)} copy-done((f32[6]{0:T(128)S(1)}, f32[6]{0:T(128)}, u32[]{:S(2)}) %copy-start.2) | copy-done | bytes 48
  3.5 58.1 %shard_map.50 = (f32[3456,128]{1,0:T(8,128)S(1)}, f32[80,128]{1,0:T(8,128)S(1)}) custom-call(f32[3456,128]{1,0:T(8,128)S(1)} %bitcast.21, s32[16,128]{1,0:T(8,128)S(1)} %bitcast.23, f32[6]{0:T(128)S(1)} %copy-done.2), custom_call_target="tpu_custom_call" | custom-call | tf_op jit(solution)/shard_map/pallas_call | solution.py:585
  61.6 1.2 %copy.11 = f32[216,2,1024]{2,1,0:T(2,128)} copy(f32[216,2,1024]{2,1,0:T(2,128)S(1)} %bitcast.20) | data formatting | bytes 3538944
  62.8 0.6 copy.12
Async XLA Ops:
  0.6 1.5 %copy-start = (f32[216,2,1024]{2,1,0:T(2,128)S(1)}, f32[216,2,1024]{2,1,0:T(2,128)}, u32[]{:S(2)}) copy-start(f32[216,2,1024]{2,1,0:T(2,128)} %param.3) | copy-start | bytes 5308420
  2.1 0.7 %copy-start.1 = (s32[2,1024]{1,0:T(2,128)S(1)}, s32[2,1024]{1,0:T(2,128)}, u32[]{:S(2)}) copy-start(s32[2,1024]{1,0:T(2,128)} %param.4) | copy-start | bytes 24580
  2.8 0.7 %copy-start.2 = (f32[6]{0:T(128)S(1)}, f32[6]{0:T(128)}, u32[]{:S(2)}) copy-start(f32[6]{0:T(128)} %boundary_ref.1) | copy-start | bytes 76

commit v4 on v3

--- a/solution.py
+++ b/solution.py
@@ -23,6 +23,7 @@
 PAIRS = RUN * RUN
 USED = 26
 ROWS = 32
+ORDER = (4, 3, 5, 2, 6, 1, 7)
 MESH = pl.DeviceIdType.MESH
 
 
@@ -171,7 +172,6 @@
 
 
 def kernel(
-    groups,
     digits,
     cells,
     state_ref,
@@ -188,7 +188,9 @@
     halo,
     acc,
     edge,
+    edge_part,
     got_edge,
+    edge_sum,
     part,
     got_a,
     mine,
@@ -220,27 +222,22 @@
     up = lax.rem(cell + 1, cells)
     down = lax.rem(cell + cells - 1, cells)
 
-    def peer_a(other):
-        return ((other // 2) * 16 + (row // 2 * 2 + lax.rem(other, 2)) * 2 + lo, cell)
-
-    def peer_b(other):
-        return (col * 16 + (other // 2 * 2 + lax.rem(row, 2)) * 2 + lax.rem(other, 2), cell)
+    def peer_a(other, slab):
+        return ((other // 2) * 16 + (row // 2 * 2 + lax.rem(other, 2)) * 2 + lo, slab)
+
+    def peer_b(other, slab):
+        return (col * 16 + (other // 2 * 2 + lax.rem(row, 2)) * 2 + lax.rem(other, 2), slab)
 
     loads = [
         pltpu.make_async_copy(state_ref, raw, input_sem.at[0]),
         pltpu.make_async_copy(kind_hbm, kind_ref, input_sem.at[1]),
     ]
     barrier = pltpu.get_barrier_semaphore()
-    for other in (up, down):
-        pl.semaphore_signal(barrier, inc=1, device_id=(vel, other), device_id_type=MESH)
-    if groups:
-        for k in range(1, 8):
-            pl.semaphore_signal(
-                barrier, inc=1, device_id=peer_a(lax.rem(here + k, 8)), device_id_type=MESH
-            )
-            pl.semaphore_signal(
-                barrier, inc=1, device_id=peer_b(lax.rem(there + k, 8)), device_id_type=MESH
-            )
+    greeted = [peer_a(lax.rem(here + k, 8), other) for k in range(8) for other in (up, down)]
+    greeted += [peer_a(lax.rem(here + k, 8), cell) for k in range(1, 8)]
+    greeted += [peer_b(lax.rem(there + k, 8), cell) for k in range(1, 8)]
+    for device in greeted:
+        pl.semaphore_signal(barrier, inc=1, device_id=device, device_id_type=MESH)
     for copy in loads:
         copy.start()
     for index, value in enumerate(one_dimensional_tables(points)):
@@ -335,21 +332,26 @@
 
     def send_edges(step, held):
         copies = []
+        for r in range(13):
+            for pi in range(2):
+                edge_part[step, pi, pl.ds(r, 8, stride=16), :] = edge[pi, r]
+        for k in ORDER + (0,):
+            other = lax.rem(here + k, 8)
+            for pi, slab in ((1, up), (0, down)):
+                copies.append(
+                    pltpu.make_async_remote_copy(
+                        src_ref=edge_part.at[step, pi, pl.ds(pl.multiple_of(other * 16, 16), 13)],
+                        dst_ref=got_edge.at[step, pi, here],
+                        send_sem=edge_send.at[step, pi, k],
+                        recv_sem=edge_recv.at[step, pi, k],
+                        device_id=peer_a(other, slab),
+                        device_id_type=MESH,
+                    )
+                )
         for pi, other in ((1, up), (0, down)):
             copies.append(
                 pltpu.make_async_remote_copy(
-                    src_ref=edge.at[step, pi],
-                    dst_ref=got_edge.at[step, pi],
-                    send_sem=edge_send.at[step, pi],
-                    recv_sem=edge_recv.at[step, pi],
-                    device_id=(vel, other),
-                    device_id_type=MESH,
-                )
-            )
-        for pi, other in ((1, up), (0, down)):
-            copies.append(
-                pltpu.make_async_remote_copy(
-                    src_ref=held.at[pi, pl.ds(pi * HALF, HALF)],
+                    src_ref=held.at[pl.ds(pi * HALF, HALF)],
                     dst_ref=halo.at[step, pi],
                     send_sem=halo_send.at[step, pi],
                     recv_sem=halo_recv.at[step, pi],
@@ -359,18 +361,18 @@
             )
         for copy in copies:
             copy.start()
-        return copies[:2], copies[2:]
+        return copies[:16], copies[16:]
 
     def exchange(step, phase, source, target, index, peer):
         copies = []
-        for k in (4, 3, 5, 2, 6, 1, 7):
+        for k in ORDER:
             other = lax.rem(index + k, 8)
             copy = pltpu.make_async_remote_copy(
                 src_ref=source(other),
                 dst_ref=target,
                 send_sem=send_sem.at[step, phase, k - 1],
                 recv_sem=recv_sem.at[step, phase, k - 1],
-                device_id=peer(other),
+                device_id=peer(other, cell),
                 device_id_type=MESH,
             )
             copy.start()
@@ -381,32 +383,32 @@
         return pl.ds(pl.multiple_of(index * ROWS, ROWS), count)
 
     def parameters_of(step, index, total_ref):
-        moment = [total_ref[pl.ds(2 * r, 2), :] for r in range(13)]
+        moment = [total_ref[pl.ds(r, 2, stride=13), :] for r in range(13)]
         kind = kind_ref[pl.ds(2 * index, 2), :]
         boundary = [boundary_ref[r] for r in range(6)]
         rows = step_parameters(moment, kind, boundary)
         for r in range(9 if step < STEPS - 1 else 14):
             gathered[step, pl.ds(index * ROWS + 2 * r, 2), :] = rows[r]
 
-    def all_sums(step):
+    def all_sums(step, edges):
         for r in range(13):
             for p in range(2):
-                mask = has_down if p == 0 else has_up
-                value = acc[r, p] + mask * got_edge[step, 1 - p, r]
-                part[step, pl.ds(2 * r + p, 8, stride=ROWS), :] = value
-        if not groups:
-            for index in range(8):
-                mine[step] = part[step, pl.ds(index * ROWS, USED), :]
-                parameters_of(step, index, mine.at[step])
-            return
+                part[step, pl.ds(13 * p + r, 8, stride=ROWS), :] = acc[r, p]
         copies = exchange(
             step, 0, lambda other: part.at[step, slice_rows(other, USED)], got_a.at[step, here], here, peer_a
         )
         got_a[step, here] = part[step, slice_rows(here, USED), :]
+        for copy in edges:
+            copy.wait()
+        for p in range(2):
+            from_edge = got_edge[step, 1 - p, 0]
+            for k in range(1, 8):
+                from_edge = from_edge + got_edge[step, 1 - p, k]
+            edge_sum[pl.ds(13 * p, 13), :] = from_edge * (has_down if p == 0 else has_up)
         for copy in copies:
             copy.wait()
-        total = got_a[step, 0]
-        for k in range(1, 8):
+        total = edge_sum[...]
+        for k in range(8):
             total = total + got_a[step, k]
         mine[step] = total
         copies = exchange(
@@ -457,7 +459,7 @@
         copy.wait()
     for step in range(STEPS):
         held = h_first if step == 0 else h_second
-        edge[step] = jnp.zeros(edge.shape[1:], jnp.float32)
+        edge[...] = jnp.zeros(edge.shape, jnp.float32)
         acc[...] = jnp.zeros(acc.shape, jnp.float32)
 
         def inner(i, carry, step=step, held=held):
@@ -465,42 +467,33 @@
             pi = ma // (RUN // 2)
             values = new_plane(step, i, ma, mb, pi, pi, False)
             for mc in range(RUN):
-                held[pi, i * RUN + mc] = values[mc]
-            add_moments(edge.at[step, pi], slice(None), run_sums(values), ma, mb, courant(ma, ja))
+                held[i * RUN + mc] = values[mc]
+            add_moments(edge.at[pi], slice(None), run_sums(values), ma, mb, courant(ma, ja))
             return carry
 
         lax.fori_loop(0, PAIRS, inner, 0, unroll=3)
         if step == 0:
-            pl.semaphore_wait(barrier, 16 if groups else 2)
+            pl.semaphore_wait(barrier, len(greeted))
         edges, halos = send_edges(step, held)
         if step > 0:
             for copy in halos_before:
                 copy.wait()
 
-        def outer(i, carry, step=step, held=held):
-            ma, mb = i // RUN, lax.rem(i, RUN)
-            pi = ma // (RUN // 2)
-            values = new_plane(step, i, ma, mb, 1 - pi, pi, True)
-            for mc in range(RUN):
-                held[1 - pi, i * RUN + mc] = values[mc]
-            return carry
-
-        lax.fori_loop(0, PAIRS, outer, 0, unroll=3)
-
         for half in range(2):
 
-            def transport(j, carry, half=half, held=held):
+            def transport(j, carry, half=half, step=step, held=held):
                 ma = j // (RUN // 2)
                 mb = half * (RUN // 2) + lax.rem(j, RUN // 2)
                 pi = ma // (RUN // 2)
                 i = ma * RUN + mb
                 kx, ky = courant(ma, ja), courant(mb, jb)
                 at_inner, at_outer = [], []
+                values = new_plane(step, i, ma, mb, 1 - pi, pi, True)
                 for mc in range(RUN):
                     node = i * RUN + mc
                     kz = courant(mc, jc)
                     stay = 1.0 - (kx + ky + kz)
-                    near, far = held[pi, node], held[1 - pi, node]
+                    near, far = held[node], values[mc]
 
                     def flat(value):
                         return (
@@ -517,10 +510,8 @@
                 add_moments(acc, 1 - pi, run_sums(at_outer), ma, mb, 1.0)
                 return carry
 
-            lax.fori_loop(0, PAIRS // 2, transport, 0, unroll=3)
-        for copy in edges:
-            copy.wait()
-        all_sums(step)
+            lax.fori_loop(0, PAIRS // 2, transport, 0, unroll=6)
+        all_sums(step, edges)
         build_tables(step)
         halos_before = halos
 
@@ -536,7 +527,7 @@
                 out_ref[pl.ds((i * RUN + mc) * 16 + plane, 8, stride=2), :] = values[mc]
         return carry
 
-    lax.fori_loop(0, PAIRS, last, 0)
+    lax.fori_loop(0, PAIRS, last, 0, unroll=3)
 
     final = STEPS - 1
     for p in range(2):
@@ -557,7 +548,7 @@
             return tuple(result)
 
         power = lax.fori_loop(
-            0, points, sums, tuple(jnp.zeros((8, 128), jnp.float32) for _ in range(18))
+            0, points, sums, tuple(jnp.zeros((8, 128), jnp.float32) for _ in range(18)), unroll=4
         )
         power = [power[d * 6 : d * 6 + 6] for d in range(3)]
         added = added_moments(power, amount, flow, inverse, heat)
@@ -578,12 +569,12 @@
     return array.reshape((lead, 8, 2, 128)).swapaxes(1, 2).reshape(lead, 2, 1024)
 
 
-def shards(groups, digits, cells, state_init, cell_kind, boundary_state):
+def shards(digits, cells, state_init, cell_kind, boundary_state):
     vmem = functools.partial(pl.BlockSpec, memory_space=pltpu.VMEM)
     smem = functools.partial(pl.BlockSpec, memory_space=pltpu.SMEM)
     f32 = jnp.float32
     state, macro = pl.pallas_call(
-        functools.partial(kernel, groups, digits, cells),
+        functools.partial(kernel, digits, cells),
         out_shape=(
             jax.ShapeDtypeStruct((NODES * 16, 128), f32),
             jax.ShapeDtypeStruct((80, 128), f32),
@@ -594,13 +585,15 @@
             pltpu.VMEM((16, 128), jnp.int32),
             pltpu.SMEM((3 * RUN * digits,), f32),
             pltpu.VMEM((NODES * 16, 128), f32),
-            pltpu.VMEM((2, NODES, 8, 128), f32),
-            pltpu.VMEM((2, NODES, 8, 128), f32),
+            pltpu.VMEM((NODES, 8, 128), f32),
+            pltpu.VMEM((NODES, 8, 128), f32),
             pltpu.VMEM((2, NODES, 8, 128), f32),
             pltpu.VMEM((STEPS, 2, HALF, 8, 128), f32),
             pltpu.VMEM((13, 2, 8, 128), f32),
-            pltpu.VMEM((STEPS, 2, 13, 8, 128), f32),
-            pltpu.VMEM((STEPS, 2, 13, 8, 128), f32),
+            pltpu.VMEM((2, 13, 8, 128), f32),
+            pltpu.VMEM((STEPS, 2, 8 * 16, 128), f32),
+            pltpu.VMEM((STEPS, 2, 8, 13, 128), f32),
+            pltpu.VMEM((USED, 128), f32),
             pltpu.VMEM((STEPS, 8 * ROWS, 128), f32),
             pltpu.VMEM((STEPS, 8, USED, 128), f32),
             pltpu.VMEM((STEPS, USED, 128), f32),
@@ -613,13 +606,13 @@
             pltpu.SemaphoreType.DMA((2,)),
             pltpu.SemaphoreType.DMA((STEPS, 3, 7)),
             pltpu.SemaphoreType.DMA((STEPS, 3, 7)),
-            pltpu.SemaphoreType.DMA((STEPS, 2)),
-            pltpu.SemaphoreType.DMA((STEPS, 2)),
+            pltpu.SemaphoreType.DMA((STEPS, 2, 8)),
+            pltpu.SemaphoreType.DMA((STEPS, 2, 8)),
             pltpu.SemaphoreType.DMA((STEPS, 2)),
             pltpu.SemaphoreType.DMA((STEPS, 2)),
         ],
         compiler_params=pltpu.CompilerParams(
-            collective_id=0, has_side_effects=True, vmem_limit_bytes=40 * 1024 * 1024
+            collective_id=0, has_side_effects=True, vmem_limit_bytes=52 * 1024 * 1024
         ),
     )(interleaved(state_init), interleaved(cell_kind), boundary_state)
     return restored(state, NODES), restored(macro, 5)
@@ -628,5 +621,5 @@
 def solution(mesh):
     in_specs = (P("vel", "cell", None), P("cell", None), P())
     out_specs = (P("vel", "cell", None), P(None, "cell", None))
-    body = functools.partial(shards, True, 4, 8)
+    body = functools.partial(shards, 4, 8)
     return jax.shard_map(body, mesh=mesh, in_specs=in_specs, out_specs=out_specs, check_vma=False)

time: 64.1 us -> 60.2 us (0.939)
  the two profiles are of different devices: /device:TPU:1 before, /device:TPU:2 now
where the time goes in v4:
time: 60.2 us; the launch traced here: 60 us
  Pallas kernels  56.1 us (93%)
  local copies, waits for them, and re-layouts  3.17 us (5%)
  between operations  0.65 us (1%)
    pallas_call x1, Pallas kernels, shards(): pl.pallas_call(functools.partial(kernel, digits, cells), out_shape=(jax.S...  56.1 us
    unnamed x6, local copies, waits for them, and re-layouts  3.17 us

profile of v4, /device:TPU:2, one launch (start us, length us, event | category | flops | bytes accessed | tf_op | source)
XLA Modules:
  0.0 60.0 jit_solution(2452088696409471344)
XLA Ops:
  0.6 0.0 copy-start
  0.6 0.7 %copy-done = s32[2,1024]{1,0:T(2,128)S(1)} copy-done((s32[2,1024]{1,0:T(2,128)S(1)}, s32[2,1024]{1,0:T(2,128)}, u32[]{:S(2)}) %copy-start) | copy-done | bytes 8216
  1.3 0.0 copy-start.1
  1.3 0.7 %copy-done.1 = f32[6]{0:T(128)S(1)} copy-done((f32[6]{0:T(128)S(1)}, f32[6]{0:T(128)}, u32[]{:S(2)}) %copy-start.1) | copy-done | bytes 48
  2.0 56.1 %shard_map.50 = (f32[3456,128]{1,0:T(8,128)S(1)}, f32[80,128]{1,0:T(8,128)S(1)}) custom-call(f32[3456,128]{1,0:T(8,128)} %bitcast.23, s32[16,128]{1,0:T(8,128)S(1)} %bitcast.22, f32[6]{0:T(128)S(1)} %copy-done.1), custom_call_target="tpu_custom_call" | custom-call | tf_op jit(solution)/shard_map/pallas_call | solution.py:576
  58.1 1.2 %copy.11 = f32[216,2,1024]{2,1,0:T(2,128)} copy(f32[216,2,1024]{2,1,0:T(2,128)S(1)} %bitcast.20) | data formatting | bytes 3538944
  59.3 0.6 %copy.12 = f32[5,2,1024]{2,1,0:T(2,128)} copy(f32[5,2,1024]{2,1,0:T(2,128)S(1)} %bitcast.21) | data formatting | bytes 81920
Async XLA Ops:
  0.6 0.7 %copy-start = (s32[2,1024]{1,0:T(2,128)S(1)}, s32[2,1024]{1,0:T(2,128)}, u32[]{:S(2)}) copy-start(s32[2,1024]{1,0:T(2,128)} %param.4) | copy-start | bytes 24580
  1.3 0.7 %copy-start.1 = (f32[6]{0:T(128)S(1)}, f32[6]{0:T(128)}, u32[]{:S(2)}) copy-start(f32[6]{0:T(128)} %boundary_ref.1) | copy-start | bytes 76

commit v5 on v4

--- a/solution.py
+++ b/solution.py
@@ -20,6 +20,7 @@
 
 NODES = RUN * RUN * RUN
 HALF = NODES // 2
+EARLY = 88
 PAIRS = RUN * RUN
 USED = 26
 ROWS = 32
@@ -271,27 +272,39 @@
             sums = terms if sums is None else [x + y for x, y in zip(sums, terms)]
         return sums
 
-    def add_moments(ref, place, sums, ma, mb, factor):
-        sx, sy = speed(ma, ja), speed(mb, jb)
-        w = weight(ma, ja) * weight(mb, jb) * factor
-        wx, wy = w * sx, w * sy
-        t0, t1, t2, t3 = sums
-        plane_square = sx * sx + sy * sy
-        both = plane_square * t0 + t2
+    def add_run(total, values, mb):
+        sy, w = speed(mb, jb), weight(mb, jb)
+        result = []
+        for n, term in enumerate(run_sums(values)):
+            term = w * term
+            row = [term]
+            for _ in range(3 - n):
+                term = sy * term
+                row.append(term)
+            if total is not None:
+                row = [x + y for x, y in zip(total[n], row)]
+            result.append(row)
+        return result
+
+    def add_moments(ref, place, total, ma, factor):
+        sx = speed(ma, ja)
+        w = weight(ma, ja) * factor
+        wx, square = w * sx, sx * sx
+        (z0, z0y, z0yy, z0yyy), (z1, z1y, z1yy), (z2, z2y), (z3,) = total
         rows = [
-            w * t0,
-            wx * t0,
-            wy * t0,
-            w * t1,
-            (wx * sx) * t0,
-            (wy * sy) * t0,
-            w * t2,
-            (wx * sy) * t0,
-            wx * t1,
-            wy * t1,
-            wx * both,
-            wy * both,
-            w * (plane_square * t1 + t3),
+            w * z0,
+            wx * z0,
+            w * z0y,
+            w * z1,
+            (wx * sx) * z0,
+            w * z0yy,
+            w * z2,
+            wx * z0y,
+            wx * z1,
+            w * z1y,
+            wx * (square * z0 + (z0yy + z2)),
+            w * (square * z0y + (z0yyy + z2y)),
+            w * (square * z1 + (z1yy + z3)),
         ]
         for r in range(13):
             ref[r, place] += rows[r]
@@ -348,18 +361,19 @@
                         device_id_type=MESH,
                     )
                 )
-        for pi, other in ((1, up), (0, down)):
-            copies.append(
-                pltpu.make_async_remote_copy(
-                    src_ref=held.at[pl.ds(pi * HALF, HALF)],
-                    dst_ref=halo.at[step, pi],
-                    send_sem=halo_send.at[step, pi],
-                    recv_sem=halo_recv.at[step, pi],
-                    device_id=(vel, other),
-                    device_id_type=MESH,
+        for part_index, (first, count) in enumerate(((0, EARLY), (EARLY, HALF - EARLY))):
+            for pi, other in ((1, up), (0, down)):
+                copies.append(
+                    pltpu.make_async_remote_copy(
+                        src_ref=held.at[pl.ds(pi * HALF + first, count)],
+                        dst_ref=halo.at[step, pi, pl.ds(first, count)],
+                        send_sem=halo_send.at[step, part_index, pi],
+                        recv_sem=halo_recv.at[step, part_index, pi],
+                        device_id=(vel, other),
+                        device_id_type=MESH,
+                    )
                 )
-            )
-        for copy in copies:
+        for copy in copies[:18]:
             copy.start()
         return copies[:16], copies[16:]
 
@@ -390,7 +404,7 @@
         for r in range(9 if step < STEPS - 1 else 14):
             gathered[step, pl.ds(index * ROWS + 2 * r, 2), :] = rows[r]
 
-    def all_sums(step, edges):
+    def all_sums(step, edges, late):
         for r in range(13):
             for p in range(2):
                 part[step, pl.ds(13 * p + r, 8, stride=ROWS), :] = acc[r, p]
@@ -417,6 +431,8 @@
         got_b[step, there] = total
         for copy in copies:
             copy.wait()
+        for copy in late:
+            copy.start()
         total = got_b[step, 0]
         for k in range(1, 8):
             total = total + got_b[step, k]
@@ -462,16 +478,19 @@
         edge[...] = jnp.zeros(edge.shape, jnp.float32)
         acc[...] = jnp.zeros(acc.shape, jnp.float32)
 
-        def inner(i, carry, step=step, held=held):
-            ma, mb = i // RUN, lax.rem(i, RUN)
+        def inner(ma, carry, step=step, held=held):
             pi = ma // (RUN // 2)
-            values = new_plane(step, i, ma, mb, pi, pi, False)
-            for mc in range(RUN):
-                held[i * RUN + mc] = values[mc]
-            add_moments(edge.at[pi], slice(None), run_sums(values), ma, mb, courant(ma, ja))
+            total = None
+            for mb in range(RUN):
+                i = ma * RUN + mb
+                values = new_plane(step, i, ma, mb, pi, pi, False)
+                for mc in range(RUN):
+                    held[i * RUN + mc] = values[mc]
+                total = add_run(total, values, mb)
+            add_moments(edge.at[pi], slice(None), total, ma, courant(ma, ja))
             return carry
 
-        lax.fori_loop(0, PAIRS, inner, 0, unroll=3)
+        lax.fori_loop(0, RUN, inner, 0)
         if step == 0:
             pl.semaphore_wait(barrier, len(greeted))
         edges, halos = send_edges(step, held)
@@ -481,37 +500,40 @@
 
         for half in range(2):
 
-            def transport(j, carry, half=half, step=step, held=held):
-                ma = j // (RUN // 2)
-                mb = half * (RUN // 2) + lax.rem(j, RUN // 2)
+            def transport(ma, carry, half=half, step=step, held=held):
                 pi = ma // (RUN // 2)
-                i = ma * RUN + mb
-                kx, ky = courant(ma, ja), courant(mb, jb)
-                at_inner, at_outer = [], []
-                values = new_plane(step, i, ma, mb, 1 - pi, pi, True)
-                for mc in range(RUN):
-                    node = i * RUN + mc
-                    kz = courant(mc, jc)
-                    stay = 1.0 - (kx + ky + kz)
-                    near, far = held[node], values[mc]
-
-                    def flat(value):
-                        return (
-                            stay * value
-                            + ky * shift_y(value, half == 1)
-                            + kz * shift_z(value, mc >= RUN // 2)
-                        )
-
-                    at_inner.append(flat(near) + kx * far)
-                    at_outer.append(flat(far))
-                    moved[pi, node] = at_inner[-1]
-                    moved[1 - pi, node] = at_outer[-1]
-                add_moments(acc, pi, run_sums(at_inner), ma, mb, 1.0)
-                add_moments(acc, 1 - pi, run_sums(at_outer), ma, mb, 1.0)
+                kx = courant(ma, ja)
+                inner_total, outer_total = None, None
+                for mb in range(half * (RUN // 2), (half + 1) * (RUN // 2)):
+                    i = ma * RUN + mb
+                    ky = courant(mb, jb)
+                    at_inner, at_outer = [], []
+                    values = new_plane(step, i, ma, mb, 1 - pi, pi, True)
+                    for mc in range(RUN):
+                        node = i * RUN + mc
+                        kz = courant(mc, jc)
+                        stay = 1.0 - (kx + ky + kz)
+                        near, far = held[node], values[mc]
+
+                        def flat(value):
+                            return (
+                                stay * value
+                                + ky * shift_y(value, half == 1)
+                                + kz * shift_z(value, mc >= RUN // 2)
+                            )
+
+                        at_inner.append(flat(near) + kx * far)
+                        at_outer.append(flat(far))
+                        moved[pi, node] = at_inner[-1]
+                        moved[1 - pi, node] = at_outer[-1]
+                    inner_total = add_run(inner_total, at_inner, mb)
+                    outer_total = add_run(outer_total, at_outer, mb)
+                add_moments(acc, pi, inner_total, ma, 1.0)
+                add_moments(acc, 1 - pi, outer_total, ma, 1.0)
                 return carry
 
-            lax.fori_loop(0, PAIRS // 2, transport, 0, unroll=6)
-        all_sums(step, edges)
+            lax.fori_loop(0, RUN, transport, 0, unroll=2)
+        all_sums(step, edges, halos[2:])
         build_tables(step)
         halos_before = halos
 
@@ -608,8 +630,8 @@
             pltpu.SemaphoreType.DMA((STEPS, 3, 7)),
             pltpu.SemaphoreType.DMA((STEPS, 2, 8)),
             pltpu.SemaphoreType.DMA((STEPS, 2, 8)),
-            pltpu.SemaphoreType.DMA((STEPS, 2)),
-            pltpu.SemaphoreType.DMA((STEPS, 2)),
+            pltpu.SemaphoreType.DMA((STEPS, 2, 2)),
+            pltpu.SemaphoreType.DMA((STEPS, 2, 2)),
         ],
         compiler_params=pltpu.CompilerParams(
             collective_id=0, has_side_effects=True, vmem_limit_bytes=52 * 1024 * 1024

time: 60.2 us -> 58.3 us (0.968)
  the two profiles are of different devices: /device:TPU:2 before, /device:TPU:1 now
where the time goes in v5:
time: 58.3 us; the launch traced here: 58.1 us
  Pallas kernels  54.2 us (93%)
  local copies, waits for them, and re-layouts  3.17 us (5%)
  between operations  0.65 us (1%)
    pallas_call x1, Pallas kernels, shards(): pl.pallas_call(functools.partial(kernel, digits, cells), out_shape=(jax.S...  54.2 us
    unnamed x6, local copies, waits for them, and re-layouts  3.17 us

profile of v5, /device:TPU:1, one launch (start us, length us, event | category | flops | bytes accessed | tf_op | source)
XLA Modules:
  0.0 58.1 jit_solution(7684940134395837631)
XLA Ops:
  0.6 0.0 copy-start
  0.6 0.7 %copy-done = s32[2,1024]{1,0:T(2,128)S(1)} copy-done((s32[2,1024]{1,0:T(2,128)S(1)}, s32[2,1024]{1,0:T(2,128)}, u32[]{:S(2)}) %copy-start) | copy-done | bytes 8216
  1.3 0.0 copy-start.1
  1.3 0.7 %copy-done.1 = f32[6]{0:T(128)S(1)} copy-done((f32[6]{0:T(128)S(1)}, f32[6]{0:T(128)}, u32[]{:S(2)}) %copy-start.1) | copy-done | bytes 48
  2.0 54.2 %shard_map.50 = (f32[3456,128]{1,0:T(8,128)S(1)}, f32[80,128]{1,0:T(8,128)S(1)}) custom-call(f32[3456,128]{1,0:T(8,128)} %bitcast.23, s32[16,128]{1,0:T(8,128)S(1)} %bitcast.22, f32[6]{0:T(128)S(1)} %copy-done.1), custom_call_target="tpu_custom_call" | custom-call | tf_op jit(solution)/shard_map/pallas_call | solution.py:598
  56.2 1.2 %copy.11 = f32[216,2,1024]{2,1,0:T(2,128)} copy(f32[216,2,1024]{2,1,0:T(2,128)S(1)} %bitcast.20) | data formatting | bytes 3538944
  57.5 0.6 %copy.12 = f32[5,2,1024]{2,1,0:T(2,128)} copy(f32[5,2,1024]{2,1,0:T(2,128)S(1)} %bitcast.21) | data formatting | bytes 81920
Async XLA Ops:
  0.6 0.7 %copy-start = (s32[2,1024]{1,0:T(2,128)S(1)}, s32[2,1024]{1,0:T(2,128)}, u32[]{:S(2)}) copy-start(s32[2,1024]{1,0:T(2,128)} %param.4) | copy-start | bytes 24580
  1.3 0.7 %copy-start.1 = (f32[6]{0:T(128)S(1)}, f32[6]{0:T(128)}, u32[]{:S(2)}) copy-start(f32[6]{0:T(128)} %boundary_ref.1) | copy-start | bytes 76

commit v6 on v5

--- a/solution.py
+++ b/solution.py
@@ -537,20 +537,6 @@
         build_tables(step)
         halos_before = halos
 
-    for copy in halos_before:
-        copy.wait()
-
-    def last(i, carry):
-        ma, mb = i // RUN, lax.rem(i, RUN)
-        pi = ma // (RUN // 2)
-        for plane, is_outer in ((pi, 0), (1 - pi, STEPS)):
-            values = relaxed(i, ma, mb, plane, pi, is_outer)
-            for mc in range(RUN):
-                out_ref[pl.ds((i * RUN + mc) * 16 + plane, 8, stride=2), :] = values[mc]
-        return carry
-
-    lax.fori_loop(0, PAIRS, last, 0, unroll=3)
-
     final = STEPS - 1
     for p in range(2):
         keep, amount, ux, uy, uz, inverse, qx, qy, qz, *old = [
@@ -580,6 +566,20 @@
         result = [density] + u + [(trace / density - square) / 3.0]
         for r in range(5):
             macro_ref[pl.ds(r * 16 + p, 8, stride=2), :] = result[r]
+
+    for copy in halos_before:
+        copy.wait()
+
+    def last(i, carry):
+        ma, mb = i // RUN, lax.rem(i, RUN)
+        pi = ma // (RUN // 2)
+        for plane, is_outer in ((pi, 0), (1 - pi, STEPS)):
+            values = relaxed(i, ma, mb, plane, pi, is_outer)
+            for mc in range(RUN):
+                out_ref[pl.ds((i * RUN + mc) * 16 + plane, 8, stride=2), :] = values[mc]
+        return carry
+
+    lax.fori_loop(0, PAIRS, last, 0, unroll=3)
 
 
 def interleaved(array):

time: 58.3 us -> 57.7 us (0.990)
  Pallas kernels: 54.2 us -> 53.6 us
    pallas_call x1, Pallas kernels: 54.2 us -> 53.6 us  [shards(): pl.pallas_call(functools.partial(kernel, digits, cells), out_shape=(jax.S...]
where the time goes in v6:
time: 57.7 us; the launch traced here: 57.5 us
  Pallas kernels  53.6 us (93%)
  local copies, waits for them, and re-layouts  3.17 us (5%)
  between operations  0.65 us (1%)
    pallas_call x1, Pallas kernels, shards(): pl.pallas_call(functools.partial(kernel, digits, cells), out_shape=(jax.S...  53.6 us
    unnamed x6, local copies, waits for them, and re-layouts  3.17 us

profile of v6, /device:TPU:1, one launch (start us, length us, event | category | flops | bytes accessed | tf_op | source)
XLA Modules:
  0.0 57.5 jit_solution(14960463801884453659)
XLA Ops:
  0.6 0.0 copy-start
  0.6 0.7 %copy-done = s32[2,1024]{1,0:T(2,128)S(1)} copy-done((s32[2,1024]{1,0:T(2,128)S(1)}, s32[2,1024]{1,0:T(2,128)}, u32[]{:S(2)}) %copy-start) | copy-done | bytes 8216
  1.3 0.0 copy-start.1
  1.3 0.7 %copy-done.1 = f32[6]{0:T(128)S(1)} copy-done((f32[6]{0:T(128)S(1)}, f32[6]{0:T(128)}, u32[]{:S(2)}) %copy-start.1) | copy-done | bytes 48
  2.0 53.6 %shard_map.50 = (f32[3456,128]{1,0:T(8,128)S(1)}, f32[80,128]{1,0:T(8,128)S(1)}) custom-call(f32[3456,128]{1,0:T(8,128)} %bitcast.23, s32[16,128]{1,0:T(8,128)S(1)} %bitcast.22, f32[6]{0:T(128)S(1)} %copy-done.1), custom_call_target="tpu_custom_call" | custom-call | tf_op jit(solution)/shard_map/pallas_call | solution.py:598
  55.6 1.2 %copy.11 = f32[216,2,1024]{2,1,0:T(2,128)} copy(f32[216,2,1024]{2,1,0:T(2,128)S(1)} %bitcast.20) | data formatting | bytes 3538944
  56.8 0.6 %copy.12 = f32[5,2,1024]{2,1,0:T(2,128)} copy(f32[5,2,1024]{2,1,0:T(2,128)S(1)} %bitcast.21) | data formatting | bytes 81920
Async XLA Ops:
  0.6 0.7 %copy-start = (s32[2,1024]{1,0:T(2,128)S(1)}, s32[2,1024]{1,0:T(2,128)}, u32[]{:S(2)}) copy-start(s32[2,1024]{1,0:T(2,128)} %param.4) | copy-start | bytes 24580
  1.3 0.7 %copy-start.1 = (f32[6]{0:T(128)S(1)}, f32[6]{0:T(128)}, u32[]{:S(2)}) copy-start(f32[6]{0:T(128)} %boundary_ref.1) | copy-start | bytes 76

commit v7 on v6

--- a/solution.py
+++ b/solution.py
@@ -20,7 +20,7 @@
 
 NODES = RUN * RUN * RUN
 HALF = NODES // 2
-EARLY = 88
+EARLY = 80
 PAIRS = RUN * RUN
 USED = 26
 ROWS = 32
@@ -567,19 +567,22 @@
         for r in range(5):
             macro_ref[pl.ds(r * 16 + p, 8, stride=2), :] = result[r]
 
+    def last(is_outer):
+        def body(i, carry):
+            ma, mb = i // RUN, lax.rem(i, RUN)
+            pi = ma // (RUN // 2)
+            plane = 1 - pi if is_outer else pi
+            values = relaxed(i, ma, mb, plane, pi, STEPS if is_outer else 0)
+            for mc in range(RUN):
+                out_ref[pl.ds((i * RUN + mc) * 16 + plane, 8, stride=2), :] = values[mc]
+            return carry
+
+        lax.fori_loop(0, PAIRS, body, 0, unroll=3)
+
+    last(False)
     for copy in halos_before:
         copy.wait()
-
-    def last(i, carry):
-        ma, mb = i // RUN, lax.rem(i, RUN)
-        pi = ma // (RUN // 2)
-        for plane, is_outer in ((pi, 0), (1 - pi, STEPS)):
-            values = relaxed(i, ma, mb, plane, pi, is_outer)
-            for mc in range(RUN):
-                out_ref[pl.ds((i * RUN + mc) * 16 + plane, 8, stride=2), :] = values[mc]
-        return carry
-
-    lax.fori_loop(0, PAIRS, last, 0, unroll=3)
+    last(True)
 
 
 def interleaved(array):

time: 57.7 us -> 57.5 us (level)
  no operation moved by 1% of the time
where the time goes in v7:
time: 57.5 us; the launch traced here: 57.3 us
  Pallas kernels  53.5 us (93%)
  local copies, waits for them, and re-layouts  3.17 us (6%)
  between operations  0.65 us (1%)
    pallas_call x1, Pallas kernels, shards(): pl.pallas_call(functools.partial(kernel, digits, cells), out_shape=(jax.S...  53.5 us
    unnamed x6, local copies, waits for them, and re-layouts  3.17 us

profile of v7, /device:TPU:1, one launch (start us, length us, event | category | flops | bytes accessed | tf_op | source)
XLA Modules:
  0.0 57.3 jit_solution(10784831280905943735)
XLA Ops:
  0.6 0.0 copy-start
  0.6 0.7 %copy-done = s32[2,1024]{1,0:T(2,128)S(1)} copy-done((s32[2,1024]{1,0:T(2,128)S(1)}, s32[2,1024]{1,0:T(2,128)}, u32[]{:S(2)}) %copy-start) | copy-done | bytes 8216
  1.3 0.0 copy-start.1
  1.3 0.7 %copy-done.1 = f32[6]{0:T(128)S(1)} copy-done((f32[6]{0:T(128)S(1)}, f32[6]{0:T(128)}, u32[]{:S(2)}) %copy-start.1) | copy-done | bytes 48
  2.0 53.5 %shard_map.50 = (f32[3456,128]{1,0:T(8,128)S(1)}, f32[80,128]{1,0:T(8,128)S(1)}) custom-call(f32[3456,128]{1,0:T(8,128)} %bitcast.23, s32[16,128]{1,0:T(8,128)S(1)} %bitcast.22, f32[6]{0:T(128)S(1)} %copy-done.1), custom_call_target="tpu_custom_call" | custom-call | tf_op jit(solution)/shard_map/pallas_call | solution.py:601
  55.5 1.2 %copy.11 = f32[216,2,1024]{2,1,0:T(2,128)} copy(f32[216,2,1024]{2,1,0:T(2,128)S(1)} %bitcast.20) | data formatting | bytes 3538944
  56.7 0.6 %copy.12 = f32[5,2,1024]{2,1,0:T(2,128)} copy(f32[5,2,1024]{2,1,0:T(2,128)S(1)} %bitcast.21) | data formatting | bytes 81920
Async XLA Ops:
  0.6 0.7 %copy-start = (s32[2,1024]{1,0:T(2,128)S(1)}, s32[2,1024]{1,0:T(2,128)}, u32[]{:S(2)}) copy-start(s32[2,1024]{1,0:T(2,128)} %param.4) | copy-start | bytes 24580
  1.3 0.7 %copy-start.1 = (f32[6]{0:T(128)S(1)}, f32[6]{0:T(128)}, u32[]{:S(2)}) copy-start(f32[6]{0:T(128)} %boundary_ref.1) | copy-start | bytes 76
